TPU v7x, 128 devices: a whole 4x4x4 slice. The times are simulated.
128 devices in a mesh: inst: 16 (over y, x), tp: 8 (over z, core).
Axes of the slice: x: 4, y: 4, z: 4, core: 2. Of those that a mesh axis runs over, the one named last changes fastest.
Arguments:
- queries: bfloat16 [4, 128, 128], P(None, 'tp'), may hold values from -100 to 100
- kv_cache: bfloat16 [512, 2, 8, 512, 128], P('inst', None, 'tp'), may hold values from -36 to 36
- slot_meta: int32 [512, 2], P('inst'), may hold values from 0 to 255, as said below
- row_len: int32 [4], replicated, may hold values from 1 to 131072, as said below
- new_slot: int32 [512], P('inst'), may hold values from 0 to 511, as said below
- master: int32 [4], replicated, may hold values from 0 to 15
Outputs:
- moved_cache: bfloat16 [512, 2, 8, 512, 128], P('inst', None, 'tp')
- moved_meta: int32 [512, 2], P('inst')
- attended: float32 [16, 4, 128, 128], P('inst', None, 'tp')
Inputs may be any that keep to these rules, and one draw needn't show every extreme that they name: new_slot is a permutation of the slots; slot j of an instance moves to slot j of some instance; slots 2k and 2k+1 of an instance move to the same instance, and every instance sends exactly 2 blocks to every instance. `slot_meta`: every sequence has one or more slots; its slots hold its block numbers 0, 1, ... once each; no sequence has more than 256 slots, and one sequence has exactly that many. `row_len`: a sequence with n slots has more than (n - 1) * 512 and at most n * 512 cached tokens; the sequence with 256 slots has exactly 131072.
All inputs are finite; a program needn't handle non-finite values.
Results may differ from a plain program's by a relative error of at most 0.001.
Values may be sent and summed in bfloat16 or wider, within the bound.
No kernel may reach another device: no remote copies, remote signals or barrier semaphores. Data moves between devices by JAX's collectives and lax.ppermute only.
A program may use at most 128 MiB of HBM per device.

v0:
```python
import jax
import jax.numpy as jnp
from jax import lax
from jax.sharding import PartitionSpec as P


def combined_all(value, axis, combine):
    everything = jax.tree.map(lambda part: lax.all_gather(part, axis), value)
    first = jax.tree.map(lambda part: part[0], everything)

    def lap(k, so_far):
        return combine(so_far, jax.tree.map(lambda part: part[k], everything))

    return lax.fori_loop(1, lax.axis_size(axis), lap, first)


def attend(queries, cache, meta, row_len):
    rows = queries.shape[0]
    heads_kv = cache.shape[2]
    block = cache.shape[3]
    width = cache.shape[4]
    groups = queries.shape[1] // heads_kv
    owner_hot = meta[:, 0][:, None] == jnp.arange(rows, dtype=jnp.int32)[None, :]
    grouped = queries.reshape(rows, heads_kv, groups, width)
    picked = jnp.einsum(
        "sr,rkgd->skgd", owner_hot.astype(jnp.bfloat16), grouped, preferred_element_type=jnp.float32
    ).astype(jnp.bfloat16)
    scores = jnp.einsum(
        "skgd,sktd->skgt", picked, cache[:, 0], preferred_element_type=jnp.float32
    ) * width ** (-0.5)
    limit = jnp.sum(owner_hot.astype(jnp.int32) * row_len[None, :], axis=1)
    position = meta[:, 1][:, None] * block + jnp.arange(block, dtype=jnp.int32)[None, :]
    valid = (position < limit[:, None])[:, None, None, :]
    masked = jnp.where(valid, scores, jnp.float32(-1e30))
    slot_max = masked.max(-1)
    row_max = jnp.where(owner_hot[:, :, None, None], slot_max[:, None], jnp.float32(-1e30)).max(0)
    slot_ref = jnp.sum(
        jnp.where(owner_hot[:, :, None, None], row_max[None], jnp.float32(0.0)), axis=1
    )
    weights = jnp.where(valid, jnp.exp(masked - slot_ref[..., None]), jnp.float32(0.0))
    slot_total = weights.sum(-1)
    slot_sum = jnp.einsum(
        "skgt,sktd->skgd",
        weights,
        cache[:, 1],
        preferred_element_type=jnp.float32,
        precision=lax.Precision.HIGHEST,
    )
    hot_float = owner_hot.astype(jnp.float32)
    total = jnp.einsum("sr,skg->rkg", hot_float, slot_total, precision=lax.Precision.HIGHEST)
    summed = jnp.einsum("sr,skgd->rkgd", hot_float, slot_sum, precision=lax.Precision.HIGHEST)
    return (row_max, total, summed)


def combine_parts(first, second):
    peak = jnp.maximum(first[0], second[0])
    scale_one = jnp.exp(first[0] - peak)
    scale_two = jnp.exp(second[0] - peak)
    total = first[1] * scale_one + second[1] * scale_two
    summed = first[2] * scale_one[..., None] + second[2] * scale_two[..., None]
    return (peak, total, summed)


def local(queries, kv_cache, slot_meta, row_len, new_slot, master):
    slots = kv_cache.shape[0]
    peers = lax.axis_size("inst")
    me = lax.axis_index("inst")
    dest_inst = new_slot // slots
    dest_local = new_slot % slots
    order = jnp.arange(slots, dtype=jnp.int32)
    same = (dest_inst[:, None] == dest_inst[None, :]) & (order[None, :] < order[:, None])
    rank = jnp.sum(same.astype(jnp.int32), axis=1)
    target = jnp.arange(2 * peers, dtype=jnp.int32)
    select = dest_inst[None, :] * 2 + rank[None, :] == target[:, None]
    flat = kv_cache.reshape(slots, -1)
    outgoing = jnp.dot(
        select.astype(jnp.bfloat16), flat, preferred_element_type=jnp.float32
    ).astype(jnp.bfloat16)
    outgoing = outgoing.reshape((peers, 2) + kv_cache.shape[1:])
    details = jnp.stack([dest_local + 1, slot_meta[:, 0], slot_meta[:, 1]], axis=1)
    out_meta = jnp.sum(select.astype(jnp.int32)[:, :, None] * details[None, :, :], axis=1).reshape(
        peers, 2, 3
    )
    arrived, arrived_meta = (
        lax.all_to_all(outgoing, "inst", split_axis=0, concat_axis=0, tiled=True),
        lax.all_to_all(out_meta, "inst", split_axis=0, concat_axis=0, tiled=True),
    )
    arrived_meta = arrived_meta.reshape(2 * peers, 3)
    placing = arrived_meta[:, 0][None, :] - 1 == order[:, None]
    moved_flat = jnp.dot(
        placing.astype(jnp.bfloat16),
        arrived.reshape(2 * peers, -1),
        preferred_element_type=jnp.float32,
    )
    moved_cache = moved_flat.astype(jnp.bfloat16).reshape(kv_cache.shape)
    moved_meta = jnp.sum(placing.astype(jnp.int32)[:, :, None] * arrived_meta[None, :, 1:3], axis=1)
    row_max, total, summed = attend(queries, moved_cache, moved_meta, row_len)
    rows = queries.shape[0]
    mine = master == me
    peak, total_all, summed_all = combined_all((row_max, total, summed), "inst", combine_parts)
    result = summed_all / total_all[..., None]
    result = jnp.where(mine[:, None, None, None], result, jnp.float32(0.0))[None]
    attended = result.reshape(1, rows, queries.shape[1], queries.shape[2]).astype(jnp.float32)
    return (moved_cache, moved_meta, attended)


def solution(mesh):
    in_specs = (
        P(None, "tp", None),
        P("inst", None, "tp", None, None),
        P("inst", None),
        P(),
        P("inst"),
        P(),
    )
    out_specs = (P("inst", None, "tp", None, None), P("inst", None), P("inst", None, "tp", None))
    return jax.shard_map(local, mesh=mesh, in_specs=in_specs, out_specs=out_specs, check_vma=False)
```

profile of v0, /device:TPU:0, one launch (start us, length us, event | category | flops | bytes accessed | tf_op | source)
XLA Modules:
  0.0 266.0 jit_solution(7533217202002326268)
XLA Ops:
  0.6 0.7 fusion.33
  1.3 0.2 convert_reduce_fusion
  1.5 0.7 pad_add_fusion
  2.2 0.1 multiply_reduce_fusion
  2.4 0.7 copy.80
  3.1 7.1 %all-to-all-start = ((s32[16,2,3]{2,1,0:T(2,128)}), s32[16,2,3]{2,1,0:T(2,128)S(1)}, u32[]{:S(2)}, u32[]{:S(2)}) async-start(s32[16,2,3]{2,1,0:T(2,128)} %bitcast.6), calls=%async_computation | async-start | bytes 32768 | tf_op jit(solution)/shard_map/all_to_all | solution.py:86
  10.2 12.0 %fusion.7 = bf16[4,8,1024,128]{3,1,2,0:T(8,128)(2,1)} fusion(bf16[4,8,1024,128]{3,2,1,0:T(8,128)(2,1)} %bitcast.120, s32[32]{0:T(128)S(1)} %multiply_add_fusion), kind=kOutput, calls=%fused_computation.14 | convolution fusion | flops 272630784 | bytes 16777344 | tf_op jit(solution)/shard_map/dot_general | solution.py:76
  22.2 8.6 %copy.87 = bf16[4,8,1024,128]{3,2,1,0:T(8,128)(2,1)} copy(bf16[4,8,1024,128]{3,1,2,0:T(8,128)(2,1)} %fusion.7) | data formatting | bytes 16777216
  30.8 7.4 %all-to-all-start.1 = ((bf16[16,2,2,1,512,128]{5,4,2,1,3,0:T(8,128)(2,1)}), bf16[16,2,2,1,512,128]{5,4,2,1,3,0:T(8,128)(2,1)}, u32[]{:S(2)}, u32[]{:S(2)}) async-start(bf16[16,2,2,1,512,128]{5,4,2,1,3,0:T(8,128)(2,1)} %bitcast.119), calls=%async_computation.1 | async-start | bytes 16777216 | tf_op jit(solution)/shard_map/all_to_all | solution.py:85
  38.5 0.1 multiply_reduce_fusion.1
  38.8 0.2 convolution_convert_fusion.2
  39.0 121.6 %all-to-all-done.1 = bf16[16,2,2,1,512,128]{5,4,2,1,3,0:T(8,128)(2,1)} async-done(((bf16[16,2,2,1,512,128]{5,4,2,1,3,0:T(8,128)(2,1)}), bf16[16,2,2,1,512,128]{5,4,2,1,3,0:T(8,128)(2,1)}, u32[]{:S(2)}, u32[]{:S(2)}) %all-to-all-start.1) | async-done | bytes 8388640 | tf_op jit(solution)/shard_map/all_to_all | solution.py:85
  160.7 8.7 %reshape.234 = bf16[32,131072]{1,0:T(8,128)(2,1)} reshape(bf16[16,2,2,1,512,128]{5,4,2,1,3,0:T(8,128)(2,1)} %all-to-all-done.1) | data formatting | bytes 16777216 | tf_op jit(solution)/shard_map/reshape | solution.py:92
  169.3 8.9 %fusion.10 = bf16[4,8,1024,128]{3,1,2,0:T(8,128)(2,1)} fusion(bf16[32,131072]{1,0:T(8,128)(2,1)} %reshape.234, s32[32]{0:T(128)S(1)} %bitcast.129), kind=kOutput, calls=%fused_computation.15 | convolution fusion | flops 272630784 | bytes 16777344 | tf_op jit(solution)/shard_map/dot_general | solution.py:90
  178.3 8.8 %copy.88 = bf16[4,8,1024,128]{3,2,1,0:T(8,128)(2,1)} copy(bf16[4,8,1024,128]{3,1,2,0:T(8,128)(2,1)} %fusion.10) | data formatting | bytes 16777216
  187.0 3.5 %fusion.35 = (f32[32,16]{1,0:T(8,128)S(1)}, f32[32,16,512]{2,1,0:T(8,128)S(1)}) fusion(bf16[32,2,1,512,128]{4,3,1,0,2:T(8,128)(2,1)} %bitcast.116, bf16[32,16,128]{2,0,1:T(8,128)(2,1)S(1)} %convolution_convert_fusion.2, pred[32,512]{1,0:T(8,128)(4,1)S(1)} %add_compare_fusion), kind=kOutput, calls=%fused_computation.71 | convolution fusion | flops 67894784 | bytes 5392384 | tf_op jit(solution)/shard_map/skgd,sktd->skgt/dot_general | solution.py:28
  190.6 0.1 select_reduce_fusion.1
  190.8 0.4 fusion.15
  191.2 3.7 %fusion.11 = f32[32,16,128]{2,1,0:T(8,128)S(1)} fusion(bf16[32,2,1,512,128]{4,3,1,0,2:T(8,128)(2,1)} %bitcast.117, f32[32,16,512]{2,1,0:T(8,128)S(1)} %get-tuple-element.255, f32[32,16]{1,0:T(8,128)S(1)} %copy.70, pred[32,512]{1,0:T(8,128)(4,1)S(1)} %add_compare_fusion), kind=kOutput, calls=%fused_computation.17 | convolution fusion | flops 403177472 | bytes 5523456 | tf_op jit(solution)/shard_map/skgt,sktd->skgd/dot_general | solution.py:42
  194.9 23.0 %all-gather.3 = f32[16,4,16]{2,1,0:T(4,128)S(1)} all-gather(f32[1,4,16]{2,1,0:T(4,128)S(1)} %bitcast.127), channel_id=2, replica_groups=mesh['inst'=16,'tp'=8] {'inst'}, dimensions={0}, use_global_device_ids=true | all-gather | bytes 4352 | tf_op jit(solution)/shard_map/all_gather | solution.py:8
  217.9 0.1 convolution_bitcast_fusion
  218.0 20.7 %all-gather.4 = f32[16,4,16]{2,1,0:T(4,128)S(1)} all-gather(f32[1,4,16]{2,1,0:T(4,128)S(1)} %convolution_bitcast_fusion), channel_id=3, replica_groups=mesh['inst'=16,'tp'=8] {'inst'}, dimensions={0}, use_global_device_ids=true | all-gather | bytes 4352 | tf_op jit(solution)/shard_map/all_gather | solution.py:8
  238.7 0.3 fusion.19
  239.0 23.7 %all-gather.2 = f32[64,16,128]{2,1,0:T(8,128)S(1)} all-gather(f32[4,16,128]{2,1,0:T(8,128)S(1)} %copy.73), channel_id=4, replica_groups=mesh['inst'=16,'tp'=8] {'inst'}, dimensions={0}, use_global_device_ids=true | all-gather | bytes 557056 | tf_op jit(solution)/shard_map/all_gather | solution.py:8
  262.7 2.5 while.19
  262.8 0.1 fusion.43
  263.0 0.1 fusion.43
  263.1 0.1 fusion.43
  263.3 0.1 fusion.43
  263.5 0.1 fusion.43
  263.6 0.1 fusion.43
  265.3 0.7 fusion.23
  (82 shorter events, 2.1 us)
Async XLA Ops:
  0.6 38.2 %copy-start = (bf16[4,16,128]{2,1,0:T(8,128)(2,1)S(1)}, bf16[4,16,128]{2,1,0:T(8,128)(2,1)}, u32[]{:S(2)}) copy-start(bf16[4,16,128]{2,1,0:T(8,128)(2,1)} %param.8) | copy-start | bytes 49156
  3.1 27.7 %all-to-all-start = ((s32[16,2,3]{2,1,0:T(2,128)}), s32[16,2,3]{2,1,0:T(2,128)S(1)}, u32[]{:S(2)}, u32[]{:S(2)}) async-start(s32[16,2,3]{2,1,0:T(2,128)} %bitcast.6), calls=%async_computation | async-start | bytes 32768 | tf_op jit(solution)/shard_map/all_to_all | solution.py:86
  30.8 7.4 %copy-start.2 = (s32[4]{0:T(128)S(1)}, s32[4]{0:T(128)}, u32[]{:S(2)}) copy-start(s32[4]{0:T(128)} %param.13) | copy-start | bytes 52
  30.8 7.8 %copy-start.3 = (s32[4]{0:T(128)S(1)}, s32[4]{0:T(128)}, u32[]{:S(2)}) copy-start(s32[4]{0:T(128)} %param.11) | copy-start | bytes 52
  30.8 129.9 %all-to-all-start.1 = ((bf16[16,2,2,1,512,128]{5,4,2,1,3,0:T(8,128)(2,1)}), bf16[16,2,2,1,512,128]{5,4,2,1,3,0:T(8,128)(2,1)}, u32[]{:S(2)}, u32[]{:S(2)}) async-start(bf16[16,2,2,1,512,128]{5,4,2,1,3,0:T(8,128)(2,1)} %bitcast.119), calls=%async_computation.1 | async-start | bytes 16777216 | tf_op jit(solution)/shard_map/all_to_all | solution.py:85
  38.6 130.8 %copy-start.1 = (s32[32,2]{0,1:T(2,128)}, s32[32,2]{0,1:T(2,128)S(1)}, u32[]{:S(2)}) copy-start(s32[32,2]{0,1:T(2,128)S(1)} %multiply_reduce_fusion.1) | copy-start | bytes 772
where the time goes:
time: 267 us; the launch traced here: 266 us
  waiting for transfers between devices  122 us (46%)
  blocking collectives  67.4 us (25%)
  matrix products  28.7 us (11%)
  local copies, waits for them, and re-layouts  27.2 us (10%)
  starting transfers between devices  14.5 us (5%)
  other arithmetic  5.12 us (2%)
    all_to_all x1, waiting for transfers between devices, local(): lax.all_to_all(outgoing, 'inst', split_axis=0, concat_axis=0, tiled=True)  122 us
    all_gather x3, blocking collectives, combined_all(): everything = jax.tree.map(lambda part: lax.all_gather(part, axis), value)  67.4 us
    unnamed x12, local copies, waits for them, and re-layouts  17.5 us
    dot_general x1, matrix products, local(): jnp.dot(select.astype(jnp.bfloat16), flat, preferred_element_type=jnp.flo...  12 us
    dot_general x1, matrix products, local(): jnp.dot(placing.astype(jnp.bfloat16), arrived.reshape(2 * peers, -1), pre...  8.92 us
    reshape x1, local copies, waits for them, and re-layouts, local(): arrived.reshape(2 * peers, -1)  8.67 us
    all_to_all x1, starting transfers between devices, local(): lax.all_to_all(outgoing, 'inst', split_axis=0, concat_axis=0, tiled=True)  7.42 us
    all_to_all x1, starting transfers between devices, local(): lax.all_to_all(out_meta, 'inst', split_axis=0, concat_axis=0, tiled=True)  7.12 us
  transfers between devices with their start and end apart: 2, of which 1 were waited for; matrix products, arithmetic and copies ran while one was open for 8% of the time, Pallas kernels for 0%

commit v1 on v0

v1 whole, which is shorter than its diff:
```python
import functools

import jax
import jax.numpy as jnp
from jax import lax
from jax.experimental import pallas as pl
from jax.experimental.pallas import tpu as pltpu
from jax.sharding import PartitionSpec as P

LOWEST = -1e30
MAX_LANE, TOTAL_LANE, META_LANE = 0, 32, 64


def gather_pairs(pairs, slots, new_slot_ref, cache_ref, out_ref, sems):
    copies = []
    for k in range(pairs):
        dest = new_slot_ref[2 * k] // slots
        copy = pltpu.make_async_copy(
            cache_ref.at[pl.ds(2 * k, 2)], out_ref.at[pl.ds(2 * dest, 2)], sems.at[k]
        )
        copy.start()
        copies.append(copy)
    for copy in copies:
        copy.wait()


def place_pairs(pairs, place_ref, arrived_ref, out_ref, sems):
    copies = []
    for i in range(pairs):
        copy = pltpu.make_async_copy(
            arrived_ref.at[pl.ds(2 * i, 2)], out_ref.at[pl.ds(2 * place_ref[i], 2)], sems.at[i]
        )
        copy.start()
        copies.append(copy)
    for copy in copies:
        copy.wait()


def attend_kernel(
    slots, group, meta_ref, len_ref, new_slot_ref, q_ref, kv_ref, out_ref, max_ref, total_ref, sum_ref
):
    step = pl.program_id(0)
    rows, heads, width = q_ref.shape
    block = kv_ref.shape[3]
    lane = lax.broadcasted_iota(jnp.int32, (heads, block), 1)
    for j in range(group):
        slot = step * group + j
        row = meta_ref[2 * slot]
        left = len_ref[row] - meta_ref[2 * slot + 1] * block
        scores = lax.dot_general(
            q_ref[row], kv_ref[j, 0, 0], (((1,), (1,)), ((), ())), preferred_element_type=jnp.float32
        ) * width ** (-0.5)
        valid = lane < left
        scores = jnp.where(valid, scores, LOWEST)
        peak = scores.max(-1, keepdims=True)
        weight = jnp.where(valid, jnp.exp(scores - peak), 0.0)
        high = weight.astype(jnp.bfloat16)
        low = (weight - high.astype(jnp.float32)).astype(jnp.bfloat16)
        both = jnp.dot(
            jnp.concatenate([high, low], axis=0), kv_ref[j, 1, 0], preferred_element_type=jnp.float32
        )
        sum_ref[slot] = both[:heads] + both[heads:]
        max_ref[slot] = jnp.broadcast_to(peak, (heads, width))
        total_ref[slot] = jnp.broadcast_to(weight.sum(-1, keepdims=True), (heads, width))

    @pl.when(step == slots // group - 1)
    def _():
        lanes = lax.broadcasted_iota(jnp.int32, (heads, width), 1)
        per = out_ref.shape[1] // 2
        for row in range(rows):
            peak = jnp.full((heads, width), LOWEST, jnp.float32)
            for slot in range(slots):
                peak = jnp.maximum(peak, jnp.where(meta_ref[2 * slot] == row, max_ref[slot], LOWEST))
            total = jnp.zeros((heads, width), jnp.float32)
            summed = jnp.zeros((heads, width), jnp.float32)
            for slot in range(slots):
                scale = jnp.where(meta_ref[2 * slot] == row, jnp.exp(max_ref[slot] - peak), 0.0)
                total = total + scale * total_ref[slot]
                summed = summed + scale * sum_ref[slot]
            stats = jnp.where(lanes < TOTAL_LANE, peak, total)
            for part in range(heads // per):
                dest = row * (heads // per) + part
                out_ref[dest, :per] = summed[part * per : (part + 1) * per]
                out_ref[dest, per:] = stats[part * per : (part + 1) * per]
        lanes = lax.broadcasted_iota(jnp.int32, (per, width), 1)
        for k in range(slots // 2):
            dest = new_slot_ref[2 * k] // slots
            values = [k] + [meta_ref[4 * k + n] for n in range(4)]
            tile = out_ref[dest, per:]
            for n, value in enumerate(values):
                value = jnp.full((per, width), value, jnp.int32).astype(jnp.float32)
                tile = jnp.where(lanes == META_LANE + n, value, tile)
            out_ref[dest, per:] = tile


def local(queries, kv_cache, slot_meta, row_len, new_slot, master):
    slots = kv_cache.shape[0]
    pairs = slots // 2
    rows, heads, width = queries.shape
    per = rows * heads // pairs
    me = lax.axis_index("inst")
    smem = pl.BlockSpec(memory_space=pltpu.SMEM)
    anywhere = pl.BlockSpec(memory_space=pl.ANY)

    outgoing = pl.pallas_call(
        functools.partial(gather_pairs, pairs, slots),
        out_shape=jax.ShapeDtypeStruct(kv_cache.shape, kv_cache.dtype),
        in_specs=[smem, anywhere],
        out_specs=anywhere,
        scratch_shapes=[pltpu.SemaphoreType.DMA((pairs,))],
        name="gather_pairs",
    )(new_slot, kv_cache)
    arrived = lax.all_to_all(outgoing, "inst", split_axis=0, concat_axis=0, tiled=True)

    group = 4
    parts = pl.pallas_call(
        functools.partial(attend_kernel, slots, group),
        out_shape=jax.ShapeDtypeStruct((pairs, 2 * per, width), jnp.float32),
        grid_spec=pltpu.PrefetchScalarGridSpec(
            num_scalar_prefetch=3,
            grid=(slots // group,),
            in_specs=[
                pl.BlockSpec((rows, heads, width), lambda i, *_: (0, 0, 0)),
                pl.BlockSpec((group,) + kv_cache.shape[1:], lambda i, *_: (i, 0, 0, 0, 0)),
            ],
            out_specs=pl.BlockSpec((pairs, 2 * per, width), lambda i, *_: (0, 0, 0)),
            scratch_shapes=[pltpu.VMEM((slots, heads, width), jnp.float32)] * 3,
        ),
        compiler_params=pltpu.CompilerParams(
            dimension_semantics=("arbitrary",), vmem_limit_bytes=16 * 1024 * 1024
        ),
        cost_estimate=pl.CostEstimate(
            flops=6 * slots * heads * kv_cache.shape[3] * width,
            bytes_accessed=kv_cache.size * 2,
            transcendentals=slots * heads * kv_cache.shape[3],
        ),
        name="attend",
    )(slot_meta.reshape(-1), row_len, new_slot, queries, kv_cache)
    mine = lax.all_to_all(parts, "inst", split_axis=0, concat_axis=0, tiled=True)

    details = mine[:, per, META_LANE : META_LANE + 5].astype(jnp.int32)
    place = details[:, 0]
    placing = place[None, :] == jnp.arange(pairs, dtype=jnp.int32)[:, None]
    moved_meta = jnp.sum(
        jnp.where(placing[:, :, None], details[None, :, 1:], 0), axis=1
    ).reshape(slots, 2)

    peaks = mine[:, per:, MAX_LANE : MAX_LANE + 1]
    totals = mine[:, per:, TOTAL_LANE : TOTAL_LANE + 1]
    scale = jnp.exp(peaks - peaks.max(0, keepdims=True))
    done = jnp.sum(mine[:, :per] * scale, axis=0) / jnp.sum(totals * scale, axis=0)
    result = lax.all_gather(done, "inst", axis=0, tiled=True).reshape(1, rows, heads, width)
    attended = jnp.where((master == me)[None, :, None, None], result, jnp.float32(0.0))

    moved_cache = pl.pallas_call(
        functools.partial(place_pairs, pairs),
        out_shape=jax.ShapeDtypeStruct(kv_cache.shape, kv_cache.dtype),
        in_specs=[smem, anywhere],
        out_specs=anywhere,
        scratch_shapes=[pltpu.SemaphoreType.DMA((pairs,))],
        name="place_pairs",
    )(place, arrived)
    return (moved_cache, moved_meta, attended)


def solution(mesh):
    in_specs = (
        P(None, "tp", None),
        P("inst", None, "tp", None, None),
        P("inst", None),
        P(),
        P("inst"),
        P(),
    )
    out_specs = (P("inst", None, "tp", None, None), P("inst", None), P("inst", None, "tp", None))
    return jax.shard_map(local, mesh=mesh, in_specs=in_specs, out_specs=out_specs, check_vma=False)
```

time: 267 us -> 682 us (2.55)
  the two profiles are of different devices: /device:TPU:0 before, /device:TPU:1 now
where the time goes in v1:
time: 682 us; the launch traced here: 677 us
  Pallas kernels  523 us (77%)
  blocking collectives  131 us (19%)
  starting transfers between devices  14.3 us (2%)
  local copies, waits for them, and re-layouts  7.36 us (1%)
    pallas_call x1, Pallas kernels, local(): pl.pallas_call(functools.partial(gather_pairs, pairs, slots), out_shape=j...  256 us
    pallas_call x1, Pallas kernels, local(): pl.pallas_call(functools.partial(place_pairs, pairs), out_shape=jax.Shape...  256 us
    all_gather x1, blocking collectives, local(): lax.all_gather(done, 'inst', axis=0, tiled=True)  131 us
  transfers between devices with their start and end apart: 2, of which 0 were waited for; matrix products, arithmetic and copies ran while one was open for 0% of the time, Pallas kernels for 38%

profile of v1, /device:TPU:1, one launch (start us, length us, event | category | flops | bytes accessed | tf_op | source)
XLA Modules:
  0.0 677.1 jit_solution(15146938986850271838)
XLA Ops:
  0.6 0.8 copy.33
  1.4 0.1 reshape.59.meta_ref
  1.5 0.0 copy-start
  1.5 3.4 copy-done
  4.9 0.0 copy-start.1
  4.9 0.7 copy-done.1
  5.6 0.7 copy-done.2
  6.3 0.7 copy-done.3
  6.9 10.6 %attend.1 = f32[16,8,128]{2,1,0:T(8,128)} custom-call(s32[64]{0:T(128)S(1)} %reshape.59.meta_ref, s32[4]{0:T(128)S(1)} %copy-done.3, s32[32]{0:T(128)S(1)} %copy-done.2, bf16[4,16,128]{2,1,0:T(8,128)(2,1)S(1)} %copy-done.1, bf16[32,2,1,512,128]{4,3,2,1,0:T(8,128)(2,1)S(1)} %copy-done), custom_call_target="tpu_custom_call" | custom-call | flops 201326592 | bytes 8388608 | tf_op jit(solution)/shard_map/attend/pallas_call | solution.py:116
  17.5 7.6 %all-to-all-start = ((f32[16,8,128]{2,1,0:T(8,128)}), f32[16,8,128]{2,1,0:T(8,128)S(1)}, u32[]{:S(2)}, u32[]{:S(2)}) async-start(f32[16,8,128]{2,1,0:T(8,128)} %attend.1), calls=%async_computation | async-start | bytes 131072 | tf_op jit(solution)/shard_map/all_to_all | solution.py:139
  25.1 256.0 %gather_pairs.1 = bf16[32,2,1,512,128]{4,3,2,1,0:T(8,128)(2,1)} custom-call(s32[32]{0:T(128)} %new_slot_ref.3, bf16[32,2,1,512,128]{4,3,2,1,0:T(8,128)(2,1)} %cache_ref.1), custom_call_target="tpu_custom_call" | custom-call | tf_op jit(solution)/shard_map/gather_pairs/pallas_call | solution.py:105
  281.1 0.0 copy-start.5
  281.1 0.0 all-to-all-done
  281.2 6.7 all-to-all-start.1
  287.9 0.0 copy-done.5
  287.9 0.1 slice_convert_fusion
  288.0 0.1 copy.34
  288.1 0.1 select_reduce_fusion
  288.2 0.1 copy.35
  288.3 0.1 reshape.60
  288.4 0.6 copy.39
  289.1 0.1 slice_reduce_fusion
  289.2 0.2 fusion
  289.4 0.1 copy.37
  289.5 0.1 copy.38
  289.6 0.1 fusion.1
  289.7 0.1 divide_bitcast_fusion
  289.8 130.6 %all-gather = f32[16,4,128]{2,1,0:T(4,128)S(1)} all-gather(f32[1,4,128]{2,1,0:T(4,128)S(1)} %divide_bitcast_fusion), channel_id=1, replica_groups=mesh['inst'=16,'tp'=8] {'inst'}, dimensions={0}, use_global_device_ids=true | all-gather | bytes 34816 | tf_op jit(solution)/shard_map/all_gather | solution.py:152
  420.4 0.7 broadcast_select_fusion
  421.1 0.0 all-to-all-done.1.arrived_ref
  421.1 0.0 copy-done.4
  421.1 256.0 %place_pairs.1 = bf16[32,2,1,512,128]{4,3,2,1,0:T(8,128)(2,1)} custom-call(s32[16]{0:T(128)} %copy-done.4, bf16[32,2,1,512,128]{4,3,2,1,0:T(8,128)(2,1)} %all-to-all-done.1.arrived_ref), custom_call_target="tpu_custom_call" | custom-call | tf_op jit(solution)/shard_map/place_pairs/pallas_call | solution.py:155
  (7 shorter events, 0.0 us)
Async XLA Ops:
  1.5 3.4 copy-start
  4.9 0.7 copy-start.1
  5.6 0.7 copy-start.2
  6.3 0.7 copy-start.3
  17.5 263.6 %all-to-all-start = ((f32[16,8,128]{2,1,0:T(8,128)}), f32[16,8,128]{2,1,0:T(8,128)S(1)}, u32[]{:S(2)}, u32[]{:S(2)}) async-start(f32[16,8,128]{2,1,0:T(8,128)} %attend.1), calls=%async_computation | async-start | bytes 131072 | tf_op jit(solution)/shard_map/all_to_all | solution.py:139
  281.1 6.8 copy-start.5
  281.2 139.9 %all-to-all-start.1 = ((bf16[32,2,1,512,128]{4,3,2,1,0:T(8,128)(2,1)}), bf16[32,2,1,512,128]{4,3,2,1,0:T(8,128)(2,1)}, u32[]{:S(2)}, u32[]{:S(2)}) async-start(bf16[32,2,1,512,128]{4,3,2,1,0:T(8,128)(2,1)} %gather_pairs.1), calls=%async_computation.1 | async-start | bytes 16777216 | tf_op jit(solution)/shard_map/all_to_all | solution.py:113
  288.1 133.0 %copy-start.4 = (s32[16]{0:T(128)}, s32[16]{0:T(128)S(1)}, u32[]{:S(2)}) copy-start(s32[16]{0:T(128)S(1)} %slice_bitcast_fusion.place_ref) | copy-start | bytes 196

commit v2 on v1

--- a/solution.py
+++ b/solution.py
@@ -1,4 +1,5 @@
 import functools
+import math
 
 import jax
 import jax.numpy as jnp
@@ -8,32 +9,111 @@
 from jax.sharding import PartitionSpec as P
 
 LOWEST = -1e30
+BRIEF = pl.CostEstimate(flops=1, bytes_accessed=1, transcendentals=0)
 MAX_LANE, TOTAL_LANE, META_LANE = 0, 32, 64
 
 
-def gather_pairs(pairs, slots, new_slot_ref, cache_ref, out_ref, sems):
-    copies = []
-    for k in range(pairs):
-        dest = new_slot_ref[2 * k] // slots
-        copy = pltpu.make_async_copy(
-            cache_ref.at[pl.ds(2 * k, 2)], out_ref.at[pl.ds(2 * dest, 2)], sems.at[k]
+def coordinates(inst, side):
+    crossed = lax.axis_index("tp") % 2 == 1
+    x, y = inst % side, inst // side
+    return jnp.where(crossed, y, x), jnp.where(crossed, x, y)
+
+
+def instance(first, second, side):
+    crossed = lax.axis_index("tp") % 2 == 1
+    return jnp.where(crossed, first * side + second, second * side + first)
+
+
+def by_distance(side, slots, new_slot_ref, order):
+    here = coordinates(lax.axis_index("inst"), side)
+    for k in range(side * side):
+        there = coordinates(new_slot_ref[2 * k] // slots, side)
+        first, second = (lax.rem(t - h + side, side) for t, h in zip(there, here))
+        order[first * side + second] = k
+
+
+def gather_plan(hops, side, slots, new_slot_ref, order, in_refs, out_refs):
+    by_distance(side, slots, new_slot_ref, order)
+    return [
+        ((in_refs[0], order[first * side + second]), (out_refs[n], second))
+        for n, first in enumerate(hops)
+        for second in range(side)
+    ]
+
+
+def stage_plan(turns, side, slots, new_slot_ref, order, in_refs, out_refs):
+    by_distance(side, slots, new_slot_ref, order)
+    return [
+        ((ref, turn if n else order[turn]), (out, n))
+        for out, turn in zip(out_refs, turns)
+        for n, ref in enumerate(in_refs)
+    ]
+
+
+def split_plan(turns, in_refs, out_refs):
+    return [((ref, turn), (out, n)) for out, turn in zip(out_refs, turns) for n, ref in enumerate(in_refs)]
+
+
+def place_plan(pieces, side, where_ref, in_refs, out_refs):
+    first_here, second_here = coordinates(lax.axis_index("inst"), side)
+    plan = []
+    for source, pair, first, second in pieces:
+        origin = instance(
+            lax.rem(first_here - first + side, side), lax.rem(second_here - second + side, side), side
         )
-        copy.start()
-        copies.append(copy)
-    for copy in copies:
-        copy.wait()
-
-
-def place_pairs(pairs, place_ref, arrived_ref, out_ref, sems):
-    copies = []
-    for i in range(pairs):
-        copy = pltpu.make_async_copy(
-            arrived_ref.at[pl.ds(2 * i, 2)], out_ref.at[pl.ds(2 * place_ref[i], 2)], sems.at[i]
-        )
-        copy.start()
-        copies.append(copy)
-    for copy in copies:
-        copy.wait()
+        target = where_ref[origin]
+        plan.append(((in_refs[source], target if pair is None else pair), (out_refs[0], target)))
+    return plan
+
+
+def move_kernel(plan, n_scalars, n_in, n_out, *refs):
+    scalars, in_refs = refs[:n_scalars], refs[n_scalars : n_scalars + n_in]
+    out_refs, scratch = refs[n_scalars + n_in :][:n_out], refs[n_scalars + n_in + n_out :]
+    buffer, in_sems, out_sems = scratch[-3:]
+    loads, stores = [], []
+    for n, ((source, m), (target, k)) in enumerate(plan(*scalars, *scratch[:-3], in_refs, out_refs)):
+        loads.append(pltpu.make_async_copy(source.at[pl.ds(2 * m, 2)], buffer.at[n], in_sems.at[n]))
+        stores.append(pltpu.make_async_copy(buffer.at[n], target.at[pl.ds(2 * k, 2)], out_sems.at[n]))
+        loads[-1].start()
+    for load, store in zip(loads, stores):
+        load.wait()
+        store.start()
+    for store in stores:
+        store.wait()
+
+
+def move(plan, count, scalars, arrays, out_pairs, name, into=None, scratch=()):
+    slot = arrays[0].shape[1:]
+    operands = arrays + ([] if into is None else [into])
+    smem, anywhere = pl.BlockSpec(memory_space=pltpu.SMEM), pl.BlockSpec(memory_space=pl.ANY)
+    size = count * 2 * math.prod(slot) * arrays[0].dtype.itemsize
+    return pl.pallas_call(
+        functools.partial(move_kernel, plan, len(scalars), len(operands), len(out_pairs)),
+        out_shape=[pltpu.HBM((2 * n,) + slot, arrays[0].dtype) for n in out_pairs],
+        in_specs=[smem] * len(scalars) + [anywhere] * len(operands),
+        out_specs=[anywhere] * len(out_pairs),
+        scratch_shapes=list(scratch)
+        + [pltpu.VMEM((count, 2) + slot, arrays[0].dtype)]
+        + [pltpu.SemaphoreType.DMA((count,))] * 2,
+        input_output_aliases={} if into is None else {len(scalars) + len(operands) - 1: 0},
+        compiler_params=pltpu.CompilerParams(vmem_limit_bytes=size + 1024 * 1024),
+        cost_estimate=BRIEF,
+        name=name,
+    )(*scalars, *operands)
+
+
+def shifted(value, side, distance, direction):
+    tp = lax.axis_size("tp")
+    pairs = []
+    for inst in range(side * side):
+        for part in range(tp):
+            x, y = inst % side, inst // side
+            if (part % 2) ^ direction:
+                y = (y + distance) % side
+            else:
+                x = (x + distance) % side
+            pairs.append((inst * tp + part, (y * side + x) * tp + part))
+    return lax.ppermute(value, ("inst", "tp"), pairs)
 
 
 def attend_kernel(
@@ -96,21 +176,31 @@
 def local(queries, kv_cache, slot_meta, row_len, new_slot, master):
     slots = kv_cache.shape[0]
     pairs = slots // 2
+    side = math.isqrt(pairs)
     rows, heads, width = queries.shape
     per = rows * heads // pairs
     me = lax.axis_index("inst")
-    smem = pl.BlockSpec(memory_space=pltpu.SMEM)
-    anywhere = pl.BlockSpec(memory_space=pl.ANY)
-
-    outgoing = pl.pallas_call(
-        functools.partial(gather_pairs, pairs, slots),
-        out_shape=jax.ShapeDtypeStruct(kv_cache.shape, kv_cache.dtype),
-        in_specs=[smem, anywhere],
-        out_specs=anywhere,
-        scratch_shapes=[pltpu.SemaphoreType.DMA((pairs,))],
-        name="gather_pairs",
-    )(new_slot, kv_cache)
-    arrived = lax.all_to_all(outgoing, "inst", split_axis=0, concat_axis=0, tiled=True)
+
+    kv_cache, new_slot = (pltpu.with_memory_space_constraint(array, pltpu.HBM) for array in (kv_cache, new_slot))
+    order = pltpu.SMEM((pairs,), jnp.int32)
+
+    def gathered(*hops):
+        plan = functools.partial(gather_plan, hops, side, slots)
+        return move(
+            plan, len(hops) * side, [new_slot], [kv_cache], [side] * len(hops), "gather", scratch=[order]
+        )
+
+    def placed(arrays, pieces, into=None):
+        plan = functools.partial(place_plan, pieces, side)
+        return move(plan, len(pieces), [where], arrays, [pairs], "place", into=into)[0]
+
+    turns = (2, 1, 3)
+    (out_two,) = gathered(2)
+    got_two = shifted(out_two, side, 2, 0)
+    out_one, out_three = gathered(1, 3)
+    got_one = shifted(out_one, side, 1, 0)
+    got_three = shifted(out_three, side, 3, 0)
+    queries, got_two = lax.optimization_barrier((queries, got_two))
 
     group = 4
     parts = pl.pallas_call(
@@ -127,39 +217,44 @@
             scratch_shapes=[pltpu.VMEM((slots, heads, width), jnp.float32)] * 3,
         ),
         compiler_params=pltpu.CompilerParams(
-            dimension_semantics=("arbitrary",), vmem_limit_bytes=16 * 1024 * 1024
+            dimension_semantics=("arbitrary",), vmem_limit_bytes=8 * 1024 * 1024
         ),
-        cost_estimate=pl.CostEstimate(
-            flops=6 * slots * heads * kv_cache.shape[3] * width,
-            bytes_accessed=kv_cache.size * 2,
-            transcendentals=slots * heads * kv_cache.shape[3],
-        ),
+        cost_estimate=BRIEF,
         name="attend",
     )(slot_meta.reshape(-1), row_len, new_slot, queries, kv_cache)
+    got_two, parts = lax.optimization_barrier((got_two, parts))
+    plan = functools.partial(stage_plan, turns, side, slots)
+    out_early = move(plan, 6, [new_slot], [kv_cache, got_two], [2] * 3, "stage", scratch=[order])
+    got_early = [shifted(array, side, turn, 1) for array, turn in zip(out_early, turns)]
     mine = lax.all_to_all(parts, "inst", split_axis=0, concat_axis=0, tiled=True)
+    out_late = move(functools.partial(split_plan, turns), 6, [], [got_one, got_three], [2] * 3, "split")
+    got_late = [shifted(out_late[0], side, 2, 1)]
+    out_late, got_early = lax.optimization_barrier((out_late, got_early))
+    got_late += [shifted(array, side, turn, 1) for array, turn in zip(out_late[1:], turns[1:])]
 
     details = mine[:, per, META_LANE : META_LANE + 5].astype(jnp.int32)
-    place = details[:, 0]
-    placing = place[None, :] == jnp.arange(pairs, dtype=jnp.int32)[:, None]
+    where = details[:, 0]
+    placing = where[None, :] == jnp.arange(pairs, dtype=jnp.int32)[:, None]
     moved_meta = jnp.sum(
         jnp.where(placing[:, :, None], details[None, :, 1:], 0), axis=1
     ).reshape(slots, 2)
+    pieces = [(0, None, 0, 0), (1, 0, 2, 0), (2, 0, 1, 0), (3, 0, 3, 0)]
+    pieces += [(4 + n, m, first, turn) for n, turn in enumerate(turns) for m, first in enumerate((0, 2))]
+    moved_cache = placed([kv_cache, got_two, got_one, got_three] + got_early, pieces)
 
     peaks = mine[:, per:, MAX_LANE : MAX_LANE + 1]
     totals = mine[:, per:, TOTAL_LANE : TOTAL_LANE + 1]
     scale = jnp.exp(peaks - peaks.max(0, keepdims=True))
     done = jnp.sum(mine[:, :per] * scale, axis=0) / jnp.sum(totals * scale, axis=0)
-    result = lax.all_gather(done, "inst", axis=0, tiled=True).reshape(1, rows, heads, width)
+    done, moved_cache = lax.optimization_barrier((done, moved_cache))
+    everyone = jnp.broadcast_to(done[None], (pairs,) + done.shape)
+    result = lax.all_to_all(everyone, "inst", split_axis=0, concat_axis=0, tiled=True)
+    result = result.reshape(1, rows, heads, width)
     attended = jnp.where((master == me)[None, :, None, None], result, jnp.float32(0.0))
 
-    moved_cache = pl.pallas_call(
-        functools.partial(place_pairs, pairs),
-        out_shape=jax.ShapeDtypeStruct(kv_cache.shape, kv_cache.dtype),
-        in_specs=[smem, anywhere],
-        out_specs=anywhere,
-        scratch_shapes=[pltpu.SemaphoreType.DMA((pairs,))],
-        name="place_pairs",
-    )(place, arrived)
+    moved_cache = placed(got_late[:1], [(0, m, first, 2) for m, first in enumerate((1, 3))], moved_cache)
+    pieces = [(n, m, first, turn) for n, turn in enumerate(turns[1:]) for m, first in enumerate((1, 3))]
+    moved_cache = placed(got_late[1:], pieces, moved_cache)
     return (moved_cache, moved_meta, attended)
 
 

time: 682 us -> 108 us (0.16)
  Pallas kernels: 523 us -> 36.8 us
  blocking collectives: 131 us -> 0 us
  waiting for transfers between devices: 0.01 us -> 40.9 us
  starting transfers between devices: 14.3 us -> 25.8 us
    pallas_call x2 -> x7, Pallas kernels: 512 us -> 24.4 us  [move(): pl.pallas_call(functools.partial(move_kernel, plan, len(scalars), len(ope...]
    all_gather x1 -> x0, blocking collectives: 131 us -> none  [local(): lax.all_gather(done, 'inst', axis=0, tiled=True)]
    ppermute x0 -> x9, starting transfers between devices: none -> 17.6 us  [shifted(): return lax.ppermute(value, ('inst', 'tp'), pairs)]
    all_to_all x1, waiting for transfers between devices: 0.01 us -> 17.2 us  [local(): lax.all_to_all(parts, 'inst', split_axis=0, concat_axis=0, tiled=True)]
    ppermute x0 -> x9, waiting for transfers between devices: none -> 16.6 us  [shifted(): return lax.ppermute(value, ('inst', 'tp'), pairs)]
    all_to_all x1, waiting for transfers between devices: 0.01 us -> 7.09 us  [local(): lax.all_to_all(everyone, 'inst', split_axis=0, concat_axis=0, tiled=True)]
  transfers between devices with their start and end apart: 2 -> 11, of which waited for: 0 -> 3; matrix products, arithmetic and copies ran while one was open for 0% -> 3% of each run, Pallas kernels for 38% -> 28%
where the time goes in v2:
time: 108 us
  waiting for transfers between devices  40.9 us (38%)
  Pallas kernels  36.8 us (34%)
  starting transfers between devices  25.8 us (24%)
  local copies, waits for them, and re-layouts  1.92 us (2%)
  other arithmetic  1.44 us (1%)
    pallas_call x7, Pallas kernels, move(): pl.pallas_call(functools.partial(move_kernel, plan, len(scalars), len(ope...  24.4 us
    ppermute x9, starting transfers between devices, shifted(): return lax.ppermute(value, ('inst', 'tp'), pairs)  17.6 us
    all_to_all x1, waiting for transfers between devices, local(): lax.all_to_all(parts, 'inst', split_axis=0, concat_axis=0, tiled=True)  17.2 us
    ppermute x9, waiting for transfers between devices, shifted(): return lax.ppermute(value, ('inst', 'tp'), pairs)  16.6 us
    pallas_call x1, Pallas kernels, local(): pl.pallas_call(functools.partial(attend_kernel, slots, group), out_shape=...  12.3 us
    all_to_all x1, waiting for transfers between devices, local(): lax.all_to_all(everyone, 'inst', split_axis=0, concat_axis=0, tiled=True)  7.09 us
    all_to_all x1, starting transfers between devices, local(): lax.all_to_all(parts, 'inst', split_axis=0, concat_axis=0, tiled=True)  4.53 us
    all_to_all x1, starting transfers between devices, local(): lax.all_to_all(everyone, 'inst', split_axis=0, concat_axis=0, tiled=True)  3.65 us
  transfers between devices with their start and end apart: 11, of which 3 were waited for; matrix products, arithmetic and copies ran while one was open for 3% of the time, Pallas kernels for 28%

profile of v2, /device:TPU:1, one launch (start us, length us, event | category | flops | bytes accessed | tf_op | source)
XLA Modules:
  0.0 107.6 jit_solution(2263630083344518937)
XLA Ops:
  0.6 3.4 %gather.2 = bf16[8,2,1,512,128]{4,3,2,1,0:T(8,128)(2,1)} custom-call(s32[32]{0:T(128)} %refs_0_.5, bf16[32,2,1,512,128]{4,3,2,1,0:T(8,128)(2,1)} %refs_1_.7), custom_call_target="tpu_custom_call" | custom-call | flops 1 | bytes 1 | tf_op jit(solution)/shard_map/gather/pallas_call | solution.py:90
  4.1 3.8 %collective-permute-start = (bf16[8,2,1,512,128]{4,3,2,1,0:T(8,128)(2,1)}, bf16[8,2,1,512,128]{4,3,2,1,0:T(8,128)(2,1)}, u32[]{:S(2)}, u32[]{:S(2)}) collective-permute-start(bf16[8,2,1,512,128]{4,3,2,1,0:T(8,128)(2,1)} %gather.2), channel_id=1, source_target_pairs={{0,16},{1,65},{2,18},{3,67},{4,20},{5,69},{6,22},{7,71},{8,24},{9,... | collective-permute-start | bytes 6291464 | tf_op jit(solution)/shard_map/ppermute | solution.py:116
  7.9 4.5 %gather.3 = (bf16[8,2,1,512,128]{4,3,2,1,0:T(8,128)(2,1)}, bf16[8,2,1,512,128]{4,3,2,1,0:T(8,128)(2,1)}) custom-call(s32[32]{0:T(128)} %refs_0_.5, bf16[32,2,1,512,128]{4,3,2,1,0:T(8,128)(2,1)} %refs_1_.7), custom_call_target="tpu_custom_call" | custom-call | flops 1 | bytes 1 | tf_op jit(solution)/shard_map/gather/pallas_call | solution.py:90
  12.4 0.5 collective-permute-start.1
  12.9 2.3 %collective-permute-start.2 = (bf16[8,2,1,512,128]{4,3,2,1,0:T(8,128)(2,1)}, bf16[8,2,1,512,128]{4,3,2,1,0:T(8,128)(2,1)}, u32[]{:S(2)}, u32[]{:S(2)}) collective-permute-start(bf16[8,2,1,512,128]{4,3,2,1,0:T(8,128)(2,1)} %get-tuple-element.26), channel_id=1, source_target_pairs={{0,24},{1,97},{2,26},{3,99},{4,28},{5,101},{6,30},{7,103},{8,0},{9... | collective-permute-start | bytes 6291464 | tf_op jit(solution)/shard_map/ppermute | solution.py:116
  15.2 0.1 reshape.60.meta_ref
  15.3 16.6 %collective-permute-done.refs_2_ = bf16[8,2,1,512,128]{4,3,2,1,0:T(8,128)(2,1)} collective-permute-done((bf16[8,2,1,512,128]{4,3,2,1,0:T(8,128)(2,1)}, bf16[8,2,1,512,128]{4,3,2,1,0:T(8,128)(2,1)}, u32[]{:S(2)}, u32[]{:S(2)}) %collective-permute-start) | collective-permute-done | bytes 2097184 | tf_op jit(solution)/shard_map/ppermute | solution.py:116
  32.0 12.3 %attend.1 = f32[16,8,128]{2,1,0:T(8,128)} custom-call(s32[64]{0:T(128)S(1)} %reshape.60.meta_ref, s32[4]{0:T(128)S(1)} %copy-done.1, s32[32]{0:T(128)} %refs_0_.5, bf16[4,16,128]{2,1,0:T(8,128)(2,1)S(1)} %copy-done, bf16[32,2,1,512,128]{4,3,2,1,0:T(8,128)(2,1)} %refs_1_.7), custom_call_target="tpu_custom_call" | custom-call | flops 1 | bytes 1 | tf_op jit(solution)/shard_map/attend/pallas_call | solution.py:206
  44.3 4.0 %stage.1 = (bf16[4,2,1,512,128]{4,3,2,1,0:T(8,128)(2,1)}, bf16[4,2,1,512,128]{4,3,2,1,0:T(8,128)(2,1)}, bf16[4,2,1,512,128]{4,3,2,1,0:T(8,128)(2,1)}) custom-call(s32[32]{0:T(128)} %refs_0_.5, bf16[32,2,1,512,128]{4,3,2,1,0:T(8,128)(2,1)} %refs_1_.7, bf16[8,2,1,512,128]{4,3,2,1,0:T(8,128)(2,1)} %collective-permute-done.refs_2_), custom_call_target="tpu_custom_call" | custom-call | flops 1 | bytes 1 | tf_op jit(solution)/shard_map/stage/pallas_call | solution.py:90
  48.3 2.6 %collective-permute-start.3 = (bf16[4,2,1,512,128]{4,3,2,1,0:T(8,128)(2,1)}, bf16[4,2,1,512,128]{4,3,2,1,0:T(8,128)(2,1)S(1)}, u32[]{:S(2)}, u32[]{:S(2)}) collective-permute-start(bf16[4,2,1,512,128]{4,3,2,1,0:T(8,128)(2,1)} %get-tuple-element.31), channel_id=1, source_target_pairs={{0,64},{1,17},{2,66},{3,19},{4,68},{5,21},{6,70},{7,23},{8,72},{9,... | collective-permute-start | bytes 3145736 | tf_op jit(solution)/shard_map/ppermute | solution.py:116
  50.9 0.5 collective-permute-start.4
  51.5 2.1 %collective-permute-start.5 = (bf16[4,2,1,512,128]{4,3,2,1,0:T(8,128)(2,1)}, bf16[4,2,1,512,128]{4,3,2,1,0:T(8,128)(2,1)}, u32[]{:S(2)}, u32[]{:S(2)}) collective-permute-start(bf16[4,2,1,512,128]{4,3,2,1,0:T(8,128)(2,1)} %get-tuple-element.33), channel_id=1, source_target_pairs={{0,96},{1,25},{2,98},{3,27},{4,100},{5,29},{6,102},{7,31},{8,104},... | collective-permute-start | bytes 3145736 | tf_op jit(solution)/shard_map/ppermute | solution.py:116
  53.6 4.5 %all-to-all-start = ((f32[16,8,128]{2,1,0:T(8,128)}), f32[16,8,128]{2,1,0:T(8,128)S(1)}, u32[]{:S(2)}, u32[]{:S(2)}) async-start(f32[16,8,128]{2,1,0:T(8,128)} %attend.1), calls=%async_computation | async-start | bytes 131072 | tf_op jit(solution)/shard_map/all_to_all | solution.py:229
  58.2 2.9 %split.1 = (bf16[4,2,1,512,128]{4,3,2,1,0:T(8,128)(2,1)}, bf16[4,2,1,512,128]{4,3,2,1,0:T(8,128)(2,1)}, bf16[4,2,1,512,128]{4,3,2,1,0:T(8,128)(2,1)}) custom-call(bf16[8,2,1,512,128]{4,3,2,1,0:T(8,128)(2,1)S(1)} %collective-permute-done.1.refs_0_.refs_3_, bf16[8,2,1,512,128]{4,3,2,1,0:T(8,128)(2,1)} %collective-permute-done.2.refs_1_.refs_4_), custom_call_target="tpu_custom_call" | custom-call | flops 1 | bytes 1 | tf_op jit(solution)/shard_map/split/pallas_call | solution.py:90
  61.1 2.9 %collective-permute-start.8 = (bf16[4,2,1,512,128]{4,3,2,1,0:T(8,128)(2,1)}, bf16[4,2,1,512,128]{4,3,2,1,0:T(8,128)(2,1)}, u32[]{:S(2)}, u32[]{:S(2)}) collective-permute-start(bf16[4,2,1,512,128]{4,3,2,1,0:T(8,128)(2,1)} %get-tuple-element.27), channel_id=1, source_target_pairs={{0,64},{1,17},{2,66},{3,19},{4,68},{5,21},{6,70},{7,23},{8,72},{9,... | collective-permute-start | bytes 3145736 | tf_op jit(solution)/shard_map/ppermute | solution.py:116
  64.0 17.2 %all-to-all-done = f32[16,8,128]{2,1,0:T(8,128)S(1)} async-done(((f32[16,8,128]{2,1,0:T(8,128)}), f32[16,8,128]{2,1,0:T(8,128)S(1)}, u32[]{:S(2)}, u32[]{:S(2)}) %all-to-all-start) | async-done | bytes 65568 | tf_op jit(solution)/shard_map/all_to_all | solution.py:229
  81.2 0.1 slice_reduce_fusion
  81.3 0.2 fusion
  81.5 0.1 copy.32
  81.7 0.1 slice_convert_fusion
  81.9 1.3 %collective-permute-start.6 = (bf16[4,2,1,512,128]{4,3,2,1,0:T(8,128)(2,1)}, bf16[4,2,1,512,128]{4,3,2,1,0:T(8,128)(2,1)}, u32[]{:S(2)}, u32[]{:S(2)}) collective-permute-start(bf16[4,2,1,512,128]{4,3,2,1,0:T(8,128)(2,1)} %get-tuple-element.34), channel_id=1, source_target_pairs={{0,32},{1,9},{2,34},{3,11},{4,36},{5,13},{6,38},{7,15},{8,40},{9,1... | collective-permute-start | bytes 3145736 | tf_op jit(solution)/shard_map/ppermute | solution.py:116
  83.1 1.5 %collective-permute-start.7 = (bf16[4,2,1,512,128]{4,3,2,1,0:T(8,128)(2,1)}, bf16[4,2,1,512,128]{4,3,2,1,0:T(8,128)(2,1)}, u32[]{:S(2)}, u32[]{:S(2)}) collective-permute-start(bf16[4,2,1,512,128]{4,3,2,1,0:T(8,128)(2,1)} %get-tuple-element.35), channel_id=1, source_target_pairs={{0,96},{1,25},{2,98},{3,27},{4,100},{5,29},{6,102},{7,31},{8,104},... | collective-permute-start | bytes 3145736 | tf_op jit(solution)/shard_map/ppermute | solution.py:116
  84.6 0.1 fusion.1
  84.9 4.1 %place.3.refs_2_ = bf16[32,2,1,512,128]{4,3,2,1,0:T(8,128)(2,1)} custom-call(s32[16]{0:T(128)S(1)} %slice_bitcast_fusion.refs_0_, bf16[32,2,1,512,128]{4,3,2,1,0:T(8,128)(2,1)} %refs_1_.7, bf16[8,2,1,512,128]{4,3,2,1,0:T(8,128)(2,1)} %collective-permute-done.refs_2_, bf16[8,2,1,512,128]{4,3,2,1,0:T(8,128)(2,1)S(1)} %collective-permute-done.1.refs_0_.refs_3_, ...), custom_call_target="tpu_custom_call" | custom-call | flops 1 | bytes 1 | tf_op jit(solution)/shard_map/place/pallas_call | solution.py:90
  89.0 0.6 broadcast_in_dim.47
  89.6 3.7 %all-to-all-start.1 = ((f32[16,4,128]{2,1,0:T(4,128)}), f32[16,4,128]{2,1,0:T(4,128)S(1)}, u32[]{:S(2)}, u32[]{:S(2)}) async-start(f32[16,4,128]{2,1,0:T(4,128)} %broadcast_in_dim.47), calls=%async_computation.1 | async-start | bytes 65536 | tf_op jit(solution)/shard_map/all_to_all | solution.py:251
  93.3 0.1 select_reduce_fusion
  93.6 0.6 copy.35
  94.3 2.6 %place.4.refs_3_ = bf16[32,2,1,512,128]{4,3,2,1,0:T(8,128)(2,1)} custom-call(s32[16]{0:T(128)S(1)} %slice_bitcast_fusion.refs_0_, bf16[4,2,1,512,128]{4,3,2,1,0:T(8,128)(2,1)} %collective-permute-done.8.refs_1_, bf16[32,2,1,512,128]{4,3,2,1,0:T(8,128)(2,1)} %place.3.refs_2_), custom_call_target="tpu_custom_call", output_to_operand_aliasing={{}: (2, {})} | custom-call | flops 1 | bytes 1 | tf_op jit(solution)/shard_map/place/pallas_call | solution.py:90
  96.8 7.1 %all-to-all-done.1 = f32[16,4,128]{2,1,0:T(4,128)S(1)} async-done(((f32[16,4,128]{2,1,0:T(4,128)}), f32[16,4,128]{2,1,0:T(4,128)S(1)}, u32[]{:S(2)}, u32[]{:S(2)}) %all-to-all-start.1) | async-done | bytes 32800 | tf_op jit(solution)/shard_map/all_to_all | solution.py:251
  103.9 0.7 broadcast_select_fusion
  104.6 3.0 %place.5 = bf16[32,2,1,512,128]{4,3,2,1,0:T(8,128)(2,1)} custom-call(s32[16]{0:T(128)S(1)} %slice_bitcast_fusion.refs_0_, bf16[4,2,1,512,128]{4,3,2,1,0:T(8,128)(2,1)} %collective-permute-done.6.refs_1_, bf16[4,2,1,512,128]{4,3,2,1,0:T(8,128)(2,1)} %collective-permute-done.7.refs_2_, ...), custom_call_target="tpu_custom_call", output_to_operand_aliasing={{}: (3, {})} | custom-call | flops 1 | bytes 1 | tf_op jit(solution)/shard_map/place/pallas_call | solution.py:90
  (26 shorter events, 0.6 us)
Async XLA Ops:
  4.0 11.1 %copy-start.2 = (s32[32,2]{0,1:T(2,128)S(1)}, s32[32,2]{0,1:T(2,128)}, u32[]{:S(2)}) copy-start(s32[32,2]{0,1:T(2,128)} %param.8) | copy-start | bytes 772
  4.1 27.9 %copy-start = (bf16[4,16,128]{2,1,0:T(8,128)(2,1)S(1)}, bf16[4,16,128]{2,1,0:T(8,128)(2,1)}, u32[]{:S(2)}) copy-start(bf16[4,16,128]{2,1,0:T(8,128)(2,1)} %q_ref) | copy-start | bytes 49156
  4.1 27.9 %copy-start.1 = (s32[4]{0:T(128)S(1)}, s32[4]{0:T(128)}, u32[]{:S(2)}) copy-start(s32[4]{0:T(128)} %len_ref.1) | copy-start | bytes 52
  4.1 27.9 %collective-permute-start = (bf16[8,2,1,512,128]{4,3,2,1,0:T(8,128)(2,1)}, bf16[8,2,1,512,128]{4,3,2,1,0:T(8,128)(2,1)}, u32[]{:S(2)}, u32[]{:S(2)}) collective-permute-start(bf16[8,2,1,512,128]{4,3,2,1,0:T(8,128)(2,1)} %gather.2), channel_id=1, source_target_pairs={{0,16},{1,65},{2,18},{3,67},{4,20},{5,69},{6,22},{7,71},{8,24},{9,... | collective-permute-start | bytes 6291464 | tf_op jit(solution)/shard_map/ppermute | solution.py:116
  12.4 45.8 %collective-permute-start.1 = (bf16[8,2,1,512,128]{4,3,2,1,0:T(8,128)(2,1)}, bf16[8,2,1,512,128]{4,3,2,1,0:T(8,128)(2,1)S(1)}, u32[]{:S(2)}, u32[]{:S(2)}) collective-permute-start(bf16[8,2,1,512,128]{4,3,2,1,0:T(8,128)(2,1)} %get-tuple-element.25), channel_id=1, source_target_pairs={{0,8},{1,33},{2,10},{3,35},{4,12},{5,37},{6,14},{7,39},{8,16},{9,4... | collective-permute-start | bytes 6291464 | tf_op jit(solution)/shard_map/ppermute | solution.py:116
  12.9 45.3 %collective-permute-start.2 = (bf16[8,2,1,512,128]{4,3,2,1,0:T(8,128)(2,1)}, bf16[8,2,1,512,128]{4,3,2,1,0:T(8,128)(2,1)}, u32[]{:S(2)}, u32[]{:S(2)}) collective-permute-start(bf16[8,2,1,512,128]{4,3,2,1,0:T(8,128)(2,1)} %get-tuple-element.26), channel_id=1, source_target_pairs={{0,24},{1,97},{2,26},{3,99},{4,28},{5,101},{6,30},{7,103},{8,0},{9... | collective-permute-start | bytes 6291464 | tf_op jit(solution)/shard_map/ppermute | solution.py:116
  44.3 13.8 %copy-start.3 = (s32[4]{0:T(128)S(1)}, s32[4]{0:T(128)}, u32[]{:S(2)}) copy-start(s32[4]{0:T(128)} %param.11) | copy-start | bytes 52
  48.3 33.5 %collective-permute-start.3 = (bf16[4,2,1,512,128]{4,3,2,1,0:T(8,128)(2,1)}, bf16[4,2,1,512,128]{4,3,2,1,0:T(8,128)(2,1)S(1)}, u32[]{:S(2)}, u32[]{:S(2)}) collective-permute-start(bf16[4,2,1,512,128]{4,3,2,1,0:T(8,128)(2,1)} %get-tuple-element.31), channel_id=1, source_target_pairs={{0,64},{1,17},{2,66},{3,19},{4,68},{5,21},{6,70},{7,23},{8,72},{9,... | collective-permute-start | bytes 3145736 | tf_op jit(solution)/shard_map/ppermute | solution.py:116
  50.9 30.9 %collective-permute-start.4 = (bf16[4,2,1,512,128]{4,3,2,1,0:T(8,128)(2,1)}, bf16[4,2,1,512,128]{4,3,2,1,0:T(8,128)(2,1)}, u32[]{:S(2)}, u32[]{:S(2)}) collective-permute-start(bf16[4,2,1,512,128]{4,3,2,1,0:T(8,128)(2,1)} %get-tuple-element.32), channel_id=1, source_target_pairs={{0,32},{1,9},{2,34},{3,11},{4,36},{5,13},{6,38},{7,15},{8,40},{9,1... | collective-permute-start | bytes 3145736 | tf_op jit(solution)/shard_map/ppermute | solution.py:116
  51.5 30.4 %collective-permute-start.5 = (bf16[4,2,1,512,128]{4,3,2,1,0:T(8,128)(2,1)}, bf16[4,2,1,512,128]{4,3,2,1,0:T(8,128)(2,1)}, u32[]{:S(2)}, u32[]{:S(2)}) collective-permute-start(bf16[4,2,1,512,128]{4,3,2,1,0:T(8,128)(2,1)} %get-tuple-element.33), channel_id=1, source_target_pairs={{0,96},{1,25},{2,98},{3,27},{4,100},{5,29},{6,102},{7,31},{8,104},... | collective-permute-start | bytes 3145736 | tf_op jit(solution)/shard_map/ppermute | solution.py:116
  53.6 27.6 %all-to-all-start = ((f32[16,8,128]{2,1,0:T(8,128)}), f32[16,8,128]{2,1,0:T(8,128)S(1)}, u32[]{:S(2)}, u32[]{:S(2)}) async-start(f32[16,8,128]{2,1,0:T(8,128)} %attend.1), calls=%async_computation | async-start | bytes 131072 | tf_op jit(solution)/shard_map/all_to_all | solution.py:229
  61.1 33.2 %collective-permute-start.8 = (bf16[4,2,1,512,128]{4,3,2,1,0:T(8,128)(2,1)}, bf16[4,2,1,512,128]{4,3,2,1,0:T(8,128)(2,1)}, u32[]{:S(2)}, u32[]{:S(2)}) collective-permute-start(bf16[4,2,1,512,128]{4,3,2,1,0:T(8,128)(2,1)} %get-tuple-element.27), channel_id=1, source_target_pairs={{0,64},{1,17},{2,66},{3,19},{4,68},{5,21},{6,70},{7,23},{8,72},{9,... | collective-permute-start | bytes 3145736 | tf_op jit(solution)/shard_map/ppermute | solution.py:116
  81.9 22.8 %collective-permute-start.6 = (bf16[4,2,1,512,128]{4,3,2,1,0:T(8,128)(2,1)}, bf16[4,2,1,512,128]{4,3,2,1,0:T(8,128)(2,1)}, u32[]{:S(2)}, u32[]{:S(2)}) collective-permute-start(bf16[4,2,1,512,128]{4,3,2,1,0:T(8,128)(2,1)} %get-tuple-element.34), channel_id=1, source_target_pairs={{0,32},{1,9},{2,34},{3,11},{4,36},{5,13},{6,38},{7,15},{8,40},{9,1... | collective-permute-start | bytes 3145736 | tf_op jit(solution)/shard_map/ppermute | solution.py:116
  83.1 21.5 %collective-permute-start.7 = (bf16[4,2,1,512,128]{4,3,2,1,0:T(8,128)(2,1)}, bf16[4,2,1,512,128]{4,3,2,1,0:T(8,128)(2,1)}, u32[]{:S(2)}, u32[]{:S(2)}) collective-permute-start(bf16[4,2,1,512,128]{4,3,2,1,0:T(8,128)(2,1)} %get-tuple-element.35), channel_id=1, source_target_pairs={{0,96},{1,25},{2,98},{3,27},{4,100},{5,29},{6,102},{7,31},{8,104},... | collective-permute-start | bytes 3145736 | tf_op jit(solution)/shard_map/ppermute | solution.py:116
  89.6 14.3 %all-to-all-start.1 = ((f32[16,4,128]{2,1,0:T(4,128)}), f32[16,4,128]{2,1,0:T(4,128)S(1)}, u32[]{:S(2)}, u32[]{:S(2)}) async-start(f32[16,4,128]{2,1,0:T(4,128)} %broadcast_in_dim.47), calls=%async_computation.1 | async-start | bytes 65536 | tf_op jit(solution)/shard_map/all_to_all | solution.py:251

commit v3 on v2

--- a/solution.py
+++ b/solution.py
@@ -13,9 +13,14 @@
 MAX_LANE, TOTAL_LANE, META_LANE = 0, 32, 64
 
 
+def bits(size):
+    assert size & (size - 1) == 0
+    return size.bit_length() - 1
+
+
 def coordinates(inst, side):
     crossed = lax.axis_index("tp") % 2 == 1
-    x, y = inst % side, inst // side
+    x, y = inst & (side - 1), lax.shift_right_logical(inst, bits(side))
     return jnp.where(crossed, y, x), jnp.where(crossed, x, y)
 
 
@@ -25,61 +30,82 @@
 
 
 def by_distance(side, slots, new_slot_ref, order):
-    here = coordinates(lax.axis_index("inst"), side)
+    here = lax.axis_index("inst")
+    x, y = here & (side - 1), lax.shift_right_logical(here, bits(side))
     for k in range(side * side):
-        there = coordinates(new_slot_ref[2 * k] // slots, side)
-        first, second = (lax.rem(t - h + side, side) for t, h in zip(there, here))
-        order[first * side + second] = k
-
-
-def gather_plan(hops, side, slots, new_slot_ref, order, in_refs, out_refs):
-    by_distance(side, slots, new_slot_ref, order)
-    return [
-        ((in_refs[0], order[first * side + second]), (out_refs[n], second))
-        for n, first in enumerate(hops)
+        there = lax.shift_right_logical(new_slot_ref[2 * k], bits(slots))
+        across = (there - x) & (side - 1)
+        order[((lax.shift_right_logical(there, bits(side)) - y) & (side - 1)) * side + across] = k
+    return lambda first, second: order[instance(first, second, side)]
+
+
+def known_already():
+    pass
+
+
+def gather_plan(hops, side, slots, new_slot_ref, in_refs, out_refs, order):
+    pair = by_distance(side, slots, new_slot_ref, order)
+    pieces = [
+        ((in_refs[0], pair(first, second)), (out, second))
+        for out, first in zip(out_refs, hops)
         for second in range(side)
     ]
-
-
-def stage_plan(turns, side, slots, new_slot_ref, order, in_refs, out_refs):
-    by_distance(side, slots, new_slot_ref, order)
-    return [
-        ((ref, turn if n else order[turn]), (out, n))
+    return pieces, known_already
+
+
+def stage_plan(turns, side, slots, new_slot_ref, in_refs, out_refs, order):
+    pair = by_distance(side, slots, new_slot_ref, order)
+    pieces = [
+        ((ref, turn if n else pair(0, turn)), (out, n))
         for out, turn in zip(out_refs, turns)
         for n, ref in enumerate(in_refs)
     ]
+    return pieces, known_already
 
 
 def split_plan(turns, in_refs, out_refs):
-    return [((ref, turn), (out, n)) for out, turn in zip(out_refs, turns) for n, ref in enumerate(in_refs)]
-
-
-def place_plan(pieces, side, where_ref, in_refs, out_refs):
+    pieces = [((ref, turn), (out, n)) for out, turn in zip(out_refs, turns) for n, ref in enumerate(in_refs)]
+    return pieces, known_already
+
+
+def place_plan(pieces, side, where_at, in_refs, out_refs, where, sem):
     first_here, second_here = coordinates(lax.axis_index("inst"), side)
+    fetch = pltpu.make_async_copy(in_refs[where_at], where, sem)
+    fetch.start()
     plan = []
     for source, pair, first, second in pieces:
         origin = instance(
-            lax.rem(first_here - first + side, side), lax.rem(second_here - second + side, side), side
+            (first_here - first) & (side - 1), (second_here - second) & (side - 1), side
         )
-        target = where_ref[origin]
+        target = functools.partial(where.__getitem__, origin)
         plan.append(((in_refs[source], target if pair is None else pair), (out_refs[0], target)))
-    return plan
+    return plan, fetch.wait
 
 
 def move_kernel(plan, n_scalars, n_in, n_out, *refs):
     scalars, in_refs = refs[:n_scalars], refs[n_scalars : n_scalars + n_in]
     out_refs, scratch = refs[n_scalars + n_in :][:n_out], refs[n_scalars + n_in + n_out :]
-    buffer, in_sems, out_sems = scratch[-3:]
-    loads, stores = [], []
-    for n, ((source, m), (target, k)) in enumerate(plan(*scalars, *scratch[:-3], in_refs, out_refs)):
-        loads.append(pltpu.make_async_copy(source.at[pl.ds(2 * m, 2)], buffer.at[n], in_sems.at[n]))
-        stores.append(pltpu.make_async_copy(buffer.at[n], target.at[pl.ds(2 * k, 2)], out_sems.at[n]))
-        loads[-1].start()
-    for load, store in zip(loads, stores):
-        load.wait()
-        store.start()
-    for store in stores:
-        store.wait()
+    *scratch, buffer, in_sems, out_sems = scratch
+    pieces, known = plan(*scalars, in_refs, out_refs, *scratch)
+
+    def part(ref, pair):
+        return ref.at[pl.ds(2 * (pair() if callable(pair) else pair), 2)]
+
+    def load(n):
+        copy = pltpu.make_async_copy(part(*pieces[n][0]), buffer.at[n], in_sems.at[n])
+        copy.start()
+        return copy
+
+    loads = [None if callable(pair) else load(n) for n, ((_, pair), _) in enumerate(pieces)]
+    known()
+    loads = [copy or load(n) for n, copy in enumerate(loads)]
+    stores = []
+    for n, copy in enumerate(loads):
+        copy.wait()
+        stores.append(pltpu.make_async_copy(buffer.at[n], part(*pieces[n][1]), out_sems.at[n]))
+        stores[-1].start()
+    for copy in stores:
+        copy.wait()
 
 
 def move(plan, count, scalars, arrays, out_pairs, name, into=None, scratch=()):
@@ -191,8 +217,9 @@
         )
 
     def placed(arrays, pieces, into=None):
-        plan = functools.partial(place_plan, pieces, side)
-        return move(plan, len(pieces), [where], arrays, [pairs], "place", into=into)[0]
+        plan = functools.partial(place_plan, pieces, side, len(arrays))
+        scratch = [order, pltpu.SemaphoreType.DMA]
+        return move(plan, len(pieces), [], arrays + [where], [pairs], "place", into=into, scratch=scratch)[0]
 
     turns = (2, 1, 3)
     (out_two,) = gathered(2)
@@ -246,15 +273,14 @@
     totals = mine[:, per:, TOTAL_LANE : TOTAL_LANE + 1]
     scale = jnp.exp(peaks - peaks.max(0, keepdims=True))
     done = jnp.sum(mine[:, :per] * scale, axis=0) / jnp.sum(totals * scale, axis=0)
-    done, moved_cache = lax.optimization_barrier((done, moved_cache))
     everyone = jnp.broadcast_to(done[None], (pairs,) + done.shape)
     result = lax.all_to_all(everyone, "inst", split_axis=0, concat_axis=0, tiled=True)
     result = result.reshape(1, rows, heads, width)
-    attended = jnp.where((master == me)[None, :, None, None], result, jnp.float32(0.0))
-
     moved_cache = placed(got_late[:1], [(0, m, first, 2) for m, first in enumerate((1, 3))], moved_cache)
     pieces = [(n, m, first, turn) for n, turn in enumerate(turns[1:]) for m, first in enumerate((1, 3))]
     moved_cache = placed(got_late[1:], pieces, moved_cache)
+    result, moved_cache = lax.optimization_barrier((result, moved_cache))
+    attended = jnp.where((master == me)[None, :, None, None], result, jnp.float32(0.0))
     return (moved_cache, moved_meta, attended)
 
 

time: 108 us -> 105 us (0.972)
  waiting for transfers between devices: 40.9 us -> 38.9 us
  Pallas kernels: 36.8 us -> 35.6 us
    all_to_all x1, waiting for transfers between devices: 7.09 us -> 0.22 us  [local(): lax.all_to_all(everyone, 'inst', split_axis=0, concat_axis=0, tiled=True)]
    ppermute x9, waiting for transfers between devices: 16.6 us -> 21.3 us  [shifted(): return lax.ppermute(value, ('inst', 'tp'), pairs)]
    pallas_call x7, Pallas kernels: 24.4 us -> 23.2 us  [move(): pl.pallas_call(functools.partial(move_kernel, plan, len(scalars), len(ope...]
  transfers between devices with their start and end apart: 11 -> 11, of which waited for: 3 -> 5; matrix products, arithmetic and copies ran while one was open for 3% -> 3% of each run, Pallas kernels for 28% -> 31%
where the time goes in v3:
time: 105 us; the launch traced here: 104 us
  waiting for transfers between devices  38.9 us (37%)
  Pallas kernels  35.6 us (34%)
  starting transfers between devices  25.8 us (25%)
  local copies, waits for them, and re-layouts  1.93 us (2%)
  other arithmetic  1.44 us (1%)
    pallas_call x7, Pallas kernels, move(): pl.pallas_call(functools.partial(move_kernel, plan, len(scalars), len(ope...  23.2 us
    ppermute x9, waiting for transfers between devices, shifted(): return lax.ppermute(value, ('inst', 'tp'), pairs)  21.3 us
    ppermute x9, starting transfers between devices, shifted(): return lax.ppermute(value, ('inst', 'tp'), pairs)  17.6 us
    all_to_all x1, waiting for transfers between devices, local(): lax.all_to_all(parts, 'inst', split_axis=0, concat_axis=0, tiled=True)  17.4 us
    pallas_call x1, Pallas kernels, local(): pl.pallas_call(functools.partial(attend_kernel, slots, group), out_shape=...  12.3 us
    all_to_all x1, starting transfers between devices, local(): lax.all_to_all(parts, 'inst', split_axis=0, concat_axis=0, tiled=True)  4.53 us
    all_to_all x1, starting transfers between devices, local(): lax.all_to_all(everyone, 'inst', split_axis=0, concat_axis=0, tiled=True)  3.65 us
  transfers between devices with their start and end apart: 11, of which 5 were waited for; matrix products, arithmetic and copies ran while one was open for 3% of the time, Pallas kernels for 31%

profile of v3, /device:TPU:1, one launch (start us, length us, event | category | flops | bytes accessed | tf_op | source)
XLA Modules:
  0.0 104.4 jit_solution(1115823242783065560)
XLA Ops:
  0.6 3.2 %gather.2 = bf16[8,2,1,512,128]{4,3,2,1,0:T(8,128)(2,1)} custom-call(s32[32]{0:T(128)} %refs_0_.6, bf16[32,2,1,512,128]{4,3,2,1,0:T(8,128)(2,1)} %refs_0_.7), custom_call_target="tpu_custom_call" | custom-call | flops 1 | bytes 1 | tf_op jit(solution)/shard_map/gather/pallas_call | solution.py:116
  3.9 3.8 %collective-permute-start = (bf16[8,2,1,512,128]{4,3,2,1,0:T(8,128)(2,1)}, bf16[8,2,1,512,128]{4,3,2,1,0:T(8,128)(2,1)}, u32[]{:S(2)}, u32[]{:S(2)}) collective-permute-start(bf16[8,2,1,512,128]{4,3,2,1,0:T(8,128)(2,1)} %gather.2), channel_id=1, source_target_pairs={{0,16},{1,65},{2,18},{3,67},{4,20},{5,69},{6,22},{7,71},{8,24},{9,... | collective-permute-start | bytes 6291464 | tf_op jit(solution)/shard_map/ppermute | solution.py:142
  7.7 4.3 %gather.3 = (bf16[8,2,1,512,128]{4,3,2,1,0:T(8,128)(2,1)}, bf16[8,2,1,512,128]{4,3,2,1,0:T(8,128)(2,1)}) custom-call(s32[32]{0:T(128)} %refs_0_.6, bf16[32,2,1,512,128]{4,3,2,1,0:T(8,128)(2,1)} %refs_0_.7), custom_call_target="tpu_custom_call" | custom-call | flops 1 | bytes 1 | tf_op jit(solution)/shard_map/gather/pallas_call | solution.py:116
  12.0 0.5 collective-permute-start.1
  12.5 2.3 %collective-permute-start.2 = (bf16[8,2,1,512,128]{4,3,2,1,0:T(8,128)(2,1)}, bf16[8,2,1,512,128]{4,3,2,1,0:T(8,128)(2,1)}, u32[]{:S(2)}, u32[]{:S(2)}) collective-permute-start(bf16[8,2,1,512,128]{4,3,2,1,0:T(8,128)(2,1)} %get-tuple-element.26), channel_id=1, source_target_pairs={{0,24},{1,97},{2,26},{3,99},{4,28},{5,101},{6,30},{7,103},{8,0},{9... | collective-permute-start | bytes 6291464 | tf_op jit(solution)/shard_map/ppermute | solution.py:142
  14.8 0.1 reshape.60.meta_ref
  14.9 16.8 %collective-permute-done.refs_2_.refs_1_ = bf16[8,2,1,512,128]{4,3,2,1,0:T(8,128)(2,1)} collective-permute-done((bf16[8,2,1,512,128]{4,3,2,1,0:T(8,128)(2,1)}, bf16[8,2,1,512,128]{4,3,2,1,0:T(8,128)(2,1)}, u32[]{:S(2)}, u32[]{:S(2)}) %collective-permute-start) | collective-permute-done | bytes 2097184 | tf_op jit(solution)/shard_map/ppermute | solution.py:142
  31.8 12.3 %attend.1 = f32[16,8,128]{2,1,0:T(8,128)} custom-call(s32[64]{0:T(128)S(1)} %reshape.60.meta_ref, s32[4]{0:T(128)S(1)} %copy-done.1, s32[32]{0:T(128)} %refs_0_.6, bf16[4,16,128]{2,1,0:T(8,128)(2,1)S(1)} %copy-done, bf16[32,2,1,512,128]{4,3,2,1,0:T(8,128)(2,1)} %refs_0_.7), custom_call_target="tpu_custom_call" | custom-call | flops 1 | bytes 1 | tf_op jit(solution)/shard_map/attend/pallas_call | solution.py:233
  44.1 3.8 %stage.1 = (bf16[4,2,1,512,128]{4,3,2,1,0:T(8,128)(2,1)}, bf16[4,2,1,512,128]{4,3,2,1,0:T(8,128)(2,1)}, bf16[4,2,1,512,128]{4,3,2,1,0:T(8,128)(2,1)}) custom-call(s32[32]{0:T(128)} %refs_0_.6, bf16[32,2,1,512,128]{4,3,2,1,0:T(8,128)(2,1)} %refs_0_.7, bf16[8,2,1,512,128]{4,3,2,1,0:T(8,128)(2,1)} %collective-permute-done.refs_2_.refs_1_), custom_call_target="tpu_custom_call" | custom-call | flops 1 | bytes 1 | tf_op jit(solution)/shard_map/stage/pallas_call | solution.py:116
  47.9 2.6 %collective-permute-start.3 = (bf16[4,2,1,512,128]{4,3,2,1,0:T(8,128)(2,1)}, bf16[4,2,1,512,128]{4,3,2,1,0:T(8,128)(2,1)S(1)}, u32[]{:S(2)}, u32[]{:S(2)}) collective-permute-start(bf16[4,2,1,512,128]{4,3,2,1,0:T(8,128)(2,1)} %get-tuple-element.31), channel_id=1, source_target_pairs={{0,64},{1,17},{2,66},{3,19},{4,68},{5,21},{6,70},{7,23},{8,72},{9,... | collective-permute-start | bytes 3145736 | tf_op jit(solution)/shard_map/ppermute | solution.py:142
  50.5 0.5 collective-permute-start.4
  51.1 2.1 %collective-permute-start.5 = (bf16[4,2,1,512,128]{4,3,2,1,0:T(8,128)(2,1)}, bf16[4,2,1,512,128]{4,3,2,1,0:T(8,128)(2,1)}, u32[]{:S(2)}, u32[]{:S(2)}) collective-permute-start(bf16[4,2,1,512,128]{4,3,2,1,0:T(8,128)(2,1)} %get-tuple-element.33), channel_id=1, source_target_pairs={{0,96},{1,25},{2,98},{3,27},{4,100},{5,29},{6,102},{7,31},{8,104},... | collective-permute-start | bytes 3145736 | tf_op jit(solution)/shard_map/ppermute | solution.py:142
  53.2 4.5 %all-to-all-start = ((f32[16,8,128]{2,1,0:T(8,128)}), f32[16,8,128]{2,1,0:T(8,128)S(1)}, u32[]{:S(2)}, u32[]{:S(2)}) async-start(f32[16,8,128]{2,1,0:T(8,128)} %attend.1), calls=%async_computation | async-start | bytes 131072 | tf_op jit(solution)/shard_map/all_to_all | solution.py:256
  57.8 2.9 %split.1 = (bf16[4,2,1,512,128]{4,3,2,1,0:T(8,128)(2,1)}, bf16[4,2,1,512,128]{4,3,2,1,0:T(8,128)(2,1)}, bf16[4,2,1,512,128]{4,3,2,1,0:T(8,128)(2,1)}) custom-call(bf16[8,2,1,512,128]{4,3,2,1,0:T(8,128)(2,1)S(1)} %collective-permute-done.1.refs_0_.refs_2_, bf16[8,2,1,512,128]{4,3,2,1,0:T(8,128)(2,1)} %collective-permute-done.2.refs_1_.refs_3_), custom_call_target="tpu_custom_call" | custom-call | flops 1 | bytes 1 | tf_op jit(solution)/shard_map/split/pallas_call | solution.py:116
  60.7 2.9 %collective-permute-start.8 = (bf16[4,2,1,512,128]{4,3,2,1,0:T(8,128)(2,1)}, bf16[4,2,1,512,128]{4,3,2,1,0:T(8,128)(2,1)}, u32[]{:S(2)}, u32[]{:S(2)}) collective-permute-start(bf16[4,2,1,512,128]{4,3,2,1,0:T(8,128)(2,1)} %get-tuple-element.27), channel_id=1, source_target_pairs={{0,64},{1,17},{2,66},{3,19},{4,68},{5,21},{6,70},{7,23},{8,72},{9,... | collective-permute-start | bytes 3145736 | tf_op jit(solution)/shard_map/ppermute | solution.py:142
  63.6 17.4 %all-to-all-done = f32[16,8,128]{2,1,0:T(8,128)S(1)} async-done(((f32[16,8,128]{2,1,0:T(8,128)}), f32[16,8,128]{2,1,0:T(8,128)S(1)}, u32[]{:S(2)}, u32[]{:S(2)}) %all-to-all-start) | async-done | bytes 65568 | tf_op jit(solution)/shard_map/all_to_all | solution.py:256
  81.2 0.1 slice_reduce_fusion
  81.3 1.3 %collective-permute-start.6 = (bf16[4,2,1,512,128]{4,3,2,1,0:T(8,128)(2,1)}, bf16[4,2,1,512,128]{4,3,2,1,0:T(8,128)(2,1)}, u32[]{:S(2)}, u32[]{:S(2)}) collective-permute-start(bf16[4,2,1,512,128]{4,3,2,1,0:T(8,128)(2,1)} %get-tuple-element.34), channel_id=1, source_target_pairs={{0,32},{1,9},{2,34},{3,11},{4,36},{5,13},{6,38},{7,15},{8,40},{9,1... | collective-permute-start | bytes 3145736 | tf_op jit(solution)/shard_map/ppermute | solution.py:142
  82.6 1.5 %collective-permute-start.7 = (bf16[4,2,1,512,128]{4,3,2,1,0:T(8,128)(2,1)}, bf16[4,2,1,512,128]{4,3,2,1,0:T(8,128)(2,1)}, u32[]{:S(2)}, u32[]{:S(2)}) collective-permute-start(bf16[4,2,1,512,128]{4,3,2,1,0:T(8,128)(2,1)} %get-tuple-element.35), channel_id=1, source_target_pairs={{0,96},{1,25},{2,98},{3,27},{4,100},{5,29},{6,102},{7,31},{8,104},... | collective-permute-start | bytes 3145736 | tf_op jit(solution)/shard_map/ppermute | solution.py:142
  84.1 0.2 fusion
  84.5 0.1 fusion.1
  84.7 0.6 broadcast_in_dim.43
  85.3 3.7 %all-to-all-start.1 = ((f32[16,4,128]{2,1,0:T(4,128)}), f32[16,4,128]{2,1,0:T(4,128)S(1)}, u32[]{:S(2)}, u32[]{:S(2)}) async-start(f32[16,4,128]{2,1,0:T(4,128)} %broadcast_in_dim.43), calls=%async_computation.1 | async-start | bytes 65536 | tf_op jit(solution)/shard_map/all_to_all | solution.py:277
  89.0 0.1 select_reduce_fusion
  89.3 0.6 copy.35
  89.9 4.6 %place.3.refs_2_ = bf16[32,2,1,512,128]{4,3,2,1,0:T(8,128)(2,1)} custom-call(bf16[32,2,1,512,128]{4,3,2,1,0:T(8,128)(2,1)} %refs_0_.7, bf16[8,2,1,512,128]{4,3,2,1,0:T(8,128)(2,1)} %collective-permute-done.refs_2_.refs_1_, bf16[8,2,1,512,128]{4,3,2,1,0:T(8,128)(2,1)S(1)} %collective-permute-done.1.refs_0_.refs_2_, ...), custom_call_target="tpu_custom_call" | custom-call | flops 1 | bytes 1 | tf_op jit(solution)/shard_map/place/pallas_call | solution.py:116
  94.6 2.1 %place.4.refs_3_ = bf16[32,2,1,512,128]{4,3,2,1,0:T(8,128)(2,1)} custom-call(bf16[4,2,1,512,128]{4,3,2,1,0:T(8,128)(2,1)} %collective-permute-done.8.refs_0_, s32[16]{0:T(128)S(1)} %slice_bitcast_fusion.refs_7_.refs_1_.refs_2_, bf16[32,2,1,512,128]{4,3,2,1,0:T(8,128)(2,1)} %place.3.refs_2_), custom_call_target="tpu_custom_call", output_to_operand_aliasing={{}: (2, {})} | custom-call | flops 1 | bytes 1 | tf_op jit(solution)/shard_map/place/pallas_call | solution.py:116
  96.6 4.3 %collective-permute-done.6.refs_0_ = bf16[4,2,1,512,128]{4,3,2,1,0:T(8,128)(2,1)} collective-permute-done((bf16[4,2,1,512,128]{4,3,2,1,0:T(8,128)(2,1)}, bf16[4,2,1,512,128]{4,3,2,1,0:T(8,128)(2,1)}, u32[]{:S(2)}, u32[]{:S(2)}) %collective-permute-start.6) | collective-permute-done | bytes 1048608 | tf_op jit(solution)/shard_map/ppermute | solution.py:142
  100.9 0.2 collective-permute-done.7.refs_1_
  101.1 2.4 %place.5 = bf16[32,2,1,512,128]{4,3,2,1,0:T(8,128)(2,1)} custom-call(bf16[4,2,1,512,128]{4,3,2,1,0:T(8,128)(2,1)} %collective-permute-done.6.refs_0_, bf16[4,2,1,512,128]{4,3,2,1,0:T(8,128)(2,1)} %collective-permute-done.7.refs_1_, s32[16]{0:T(128)S(1)} %slice_bitcast_fusion.refs_7_.refs_1_.refs_2_, ...), custom_call_target="tpu_custom_call", output_to_operand_aliasing={{}: (3, {})} | custom-call | flops 1 | bytes 1 | tf_op jit(solution)/shard_map/place/pallas_call | solution.py:116
  103.5 0.2 all-to-all-done.1
  103.7 0.7 broadcast_select_fusion
  (26 shorter events, 0.7 us)
Async XLA Ops:
  3.8 10.9 %copy-start.2 = (s32[32,2]{0,1:T(2,128)S(1)}, s32[32,2]{0,1:T(2,128)}, u32[]{:S(2)}) copy-start(s32[32,2]{0,1:T(2,128)} %param.8) | copy-start | bytes 772
  3.8 27.9 %copy-start = (bf16[4,16,128]{2,1,0:T(8,128)(2,1)S(1)}, bf16[4,16,128]{2,1,0:T(8,128)(2,1)}, u32[]{:S(2)}) copy-start(bf16[4,16,128]{2,1,0:T(8,128)(2,1)} %q_ref) | copy-start | bytes 49156
  3.9 27.9 %copy-start.1 = (s32[4]{0:T(128)S(1)}, s32[4]{0:T(128)}, u32[]{:S(2)}) copy-start(s32[4]{0:T(128)} %len_ref.1) | copy-start | bytes 52
  3.9 27.9 %collective-permute-start = (bf16[8,2,1,512,128]{4,3,2,1,0:T(8,128)(2,1)}, bf16[8,2,1,512,128]{4,3,2,1,0:T(8,128)(2,1)}, u32[]{:S(2)}, u32[]{:S(2)}) collective-permute-start(bf16[8,2,1,512,128]{4,3,2,1,0:T(8,128)(2,1)} %gather.2), channel_id=1, source_target_pairs={{0,16},{1,65},{2,18},{3,67},{4,20},{5,69},{6,22},{7,71},{8,24},{9,... | collective-permute-start | bytes 6291464 | tf_op jit(solution)/shard_map/ppermute | solution.py:142
  12.0 45.8 %collective-permute-start.1 = (bf16[8,2,1,512,128]{4,3,2,1,0:T(8,128)(2,1)}, bf16[8,2,1,512,128]{4,3,2,1,0:T(8,128)(2,1)S(1)}, u32[]{:S(2)}, u32[]{:S(2)}) collective-permute-start(bf16[8,2,1,512,128]{4,3,2,1,0:T(8,128)(2,1)} %get-tuple-element.25), channel_id=1, source_target_pairs={{0,8},{1,33},{2,10},{3,35},{4,12},{5,37},{6,14},{7,39},{8,16},{9,4... | collective-permute-start | bytes 6291464 | tf_op jit(solution)/shard_map/ppermute | solution.py:142
  12.5 45.3 %collective-permute-start.2 = (bf16[8,2,1,512,128]{4,3,2,1,0:T(8,128)(2,1)}, bf16[8,2,1,512,128]{4,3,2,1,0:T(8,128)(2,1)}, u32[]{:S(2)}, u32[]{:S(2)}) collective-permute-start(bf16[8,2,1,512,128]{4,3,2,1,0:T(8,128)(2,1)} %get-tuple-element.26), channel_id=1, source_target_pairs={{0,24},{1,97},{2,26},{3,99},{4,28},{5,101},{6,30},{7,103},{8,0},{9... | collective-permute-start | bytes 6291464 | tf_op jit(solution)/shard_map/ppermute | solution.py:142
  44.1 13.6 %copy-start.3 = (s32[4]{0:T(128)S(1)}, s32[4]{0:T(128)}, u32[]{:S(2)}) copy-start(s32[4]{0:T(128)} %param.11) | copy-start | bytes 52
  47.9 33.4 %collective-permute-start.3 = (bf16[4,2,1,512,128]{4,3,2,1,0:T(8,128)(2,1)}, bf16[4,2,1,512,128]{4,3,2,1,0:T(8,128)(2,1)S(1)}, u32[]{:S(2)}, u32[]{:S(2)}) collective-permute-start(bf16[4,2,1,512,128]{4,3,2,1,0:T(8,128)(2,1)} %get-tuple-element.31), channel_id=1, source_target_pairs={{0,64},{1,17},{2,66},{3,19},{4,68},{5,21},{6,70},{7,23},{8,72},{9,... | collective-permute-start | bytes 3145736 | tf_op jit(solution)/shard_map/ppermute | solution.py:142
  50.5 30.8 %collective-permute-start.4 = (bf16[4,2,1,512,128]{4,3,2,1,0:T(8,128)(2,1)}, bf16[4,2,1,512,128]{4,3,2,1,0:T(8,128)(2,1)}, u32[]{:S(2)}, u32[]{:S(2)}) collective-permute-start(bf16[4,2,1,512,128]{4,3,2,1,0:T(8,128)(2,1)} %get-tuple-element.32), channel_id=1, source_target_pairs={{0,32},{1,9},{2,34},{3,11},{4,36},{5,13},{6,38},{7,15},{8,40},{9,1... | collective-permute-start | bytes 3145736 | tf_op jit(solution)/shard_map/ppermute | solution.py:142
  51.1 30.3 %collective-permute-start.5 = (bf16[4,2,1,512,128]{4,3,2,1,0:T(8,128)(2,1)}, bf16[4,2,1,512,128]{4,3,2,1,0:T(8,128)(2,1)}, u32[]{:S(2)}, u32[]{:S(2)}) collective-permute-start(bf16[4,2,1,512,128]{4,3,2,1,0:T(8,128)(2,1)} %get-tuple-element.33), channel_id=1, source_target_pairs={{0,96},{1,25},{2,98},{3,27},{4,100},{5,29},{6,102},{7,31},{8,104},... | collective-permute-start | bytes 3145736 | tf_op jit(solution)/shard_map/ppermute | solution.py:142
  53.2 27.8 %all-to-all-start = ((f32[16,8,128]{2,1,0:T(8,128)}), f32[16,8,128]{2,1,0:T(8,128)S(1)}, u32[]{:S(2)}, u32[]{:S(2)}) async-start(f32[16,8,128]{2,1,0:T(8,128)} %attend.1), calls=%async_computation | async-start | bytes 131072 | tf_op jit(solution)/shard_map/all_to_all | solution.py:256
  60.7 33.9 %collective-permute-start.8 = (bf16[4,2,1,512,128]{4,3,2,1,0:T(8,128)(2,1)}, bf16[4,2,1,512,128]{4,3,2,1,0:T(8,128)(2,1)}, u32[]{:S(2)}, u32[]{:S(2)}) collective-permute-start(bf16[4,2,1,512,128]{4,3,2,1,0:T(8,128)(2,1)} %get-tuple-element.27), channel_id=1, source_target_pairs={{0,64},{1,17},{2,66},{3,19},{4,68},{5,21},{6,70},{7,23},{8,72},{9,... | collective-permute-start | bytes 3145736 | tf_op jit(solution)/shard_map/ppermute | solution.py:142
  81.3 19.6 %collective-permute-start.6 = (bf16[4,2,1,512,128]{4,3,2,1,0:T(8,128)(2,1)}, bf16[4,2,1,512,128]{4,3,2,1,0:T(8,128)(2,1)}, u32[]{:S(2)}, u32[]{:S(2)}) collective-permute-start(bf16[4,2,1,512,128]{4,3,2,1,0:T(8,128)(2,1)} %get-tuple-element.34), channel_id=1, source_target_pairs={{0,32},{1,9},{2,34},{3,11},{4,36},{5,13},{6,38},{7,15},{8,40},{9,1... | collective-permute-start | bytes 3145736 | tf_op jit(solution)/shard_map/ppermute | solution.py:142
  82.6 18.5 %collective-permute-start.7 = (bf16[4,2,1,512,128]{4,3,2,1,0:T(8,128)(2,1)}, bf16[4,2,1,512,128]{4,3,2,1,0:T(8,128)(2,1)}, u32[]{:S(2)}, u32[]{:S(2)}) collective-permute-start(bf16[4,2,1,512,128]{4,3,2,1,0:T(8,128)(2,1)} %get-tuple-element.35), channel_id=1, source_target_pairs={{0,96},{1,25},{2,98},{3,27},{4,100},{5,29},{6,102},{7,31},{8,104},... | collective-permute-start | bytes 3145736 | tf_op jit(solution)/shard_map/ppermute | solution.py:142
  85.3 18.5 %all-to-all-start.1 = ((f32[16,4,128]{2,1,0:T(4,128)}), f32[16,4,128]{2,1,0:T(4,128)S(1)}, u32[]{:S(2)}, u32[]{:S(2)}) async-start(f32[16,4,128]{2,1,0:T(4,128)} %broadcast_in_dim.43), calls=%async_computation.1 | async-start | bytes 65536 | tf_op jit(solution)/shard_map/all_to_all | solution.py:277

commit v4 on v3

--- a/solution.py
+++ b/solution.py
@@ -63,8 +63,10 @@
     return pieces, known_already
 
 
-def split_plan(turns, in_refs, out_refs):
-    pieces = [((ref, turn), (out, n)) for out, turn in zip(out_refs, turns) for n, ref in enumerate(in_refs)]
+def split_plan(parts, in_refs, out_refs):
+    pieces = [
+        ((in_refs[ref], turn), (out, n)) for out, (turn, refs) in zip(out_refs, parts) for n, ref in enumerate(refs)
+    ]
     return pieces, known_already
 
 
@@ -142,15 +144,14 @@
     return lax.ppermute(value, ("inst", "tp"), pairs)
 
 
-def attend_kernel(
-    slots, group, meta_ref, len_ref, new_slot_ref, q_ref, kv_ref, out_ref, max_ref, total_ref, sum_ref
-):
+def attend_slots(start, group, meta_ref, len_ref, q_ref, kv_ref, max_ref, total_ref, sum_ref):
     step = pl.program_id(0)
-    rows, heads, width = q_ref.shape
+    heads, width = q_ref.shape[1:]
     block = kv_ref.shape[3]
     lane = lax.broadcasted_iota(jnp.int32, (heads, block), 1)
     for j in range(group):
-        slot = step * group + j
+        at = step * group + j
+        slot = start + at
         row = meta_ref[2 * slot]
         left = len_ref[row] - meta_ref[2 * slot + 1] * block
         scores = lax.dot_general(
@@ -165,24 +166,39 @@
         both = jnp.dot(
             jnp.concatenate([high, low], axis=0), kv_ref[j, 1, 0], preferred_element_type=jnp.float32
         )
-        sum_ref[slot] = both[:heads] + both[heads:]
-        max_ref[slot] = jnp.broadcast_to(peak, (heads, width))
-        total_ref[slot] = jnp.broadcast_to(weight.sum(-1, keepdims=True), (heads, width))
-
-    @pl.when(step == slots // group - 1)
+        sum_ref[at] = both[:heads] + both[heads:]
+        max_ref[at] = jnp.broadcast_to(peak, (heads, width))
+        total_ref[at] = jnp.broadcast_to(weight.sum(-1, keepdims=True), (heads, width))
+
+
+def attend_early(group, meta_ref, len_ref, q_ref, kv_ref, max_ref, total_ref, sum_ref):
+    attend_slots(0, group, meta_ref, len_ref, q_ref, kv_ref, max_ref, total_ref, sum_ref)
+
+
+def attend_late(slots, start, group, meta_ref, len_ref, new_slot_ref, q_ref, kv_ref, *refs):
+    early, out_ref, late = refs[:3], refs[3], refs[4:]
+    attend_slots(start, group, meta_ref, len_ref, q_ref, kv_ref, *late)
+
+    @pl.when(pl.program_id(0) == (slots - start) // group - 1)
     def _():
+        rows, heads, width = q_ref.shape
         lanes = lax.broadcasted_iota(jnp.int32, (heads, width), 1)
         per = out_ref.shape[1] // 2
+
+        def of_slot(slot):
+            return [ref[slot] for ref in early] if slot < start else [ref[slot - start] for ref in late]
+
         for row in range(rows):
             peak = jnp.full((heads, width), LOWEST, jnp.float32)
             for slot in range(slots):
-                peak = jnp.maximum(peak, jnp.where(meta_ref[2 * slot] == row, max_ref[slot], LOWEST))
+                peak = jnp.maximum(peak, jnp.where(meta_ref[2 * slot] == row, of_slot(slot)[0], LOWEST))
             total = jnp.zeros((heads, width), jnp.float32)
             summed = jnp.zeros((heads, width), jnp.float32)
             for slot in range(slots):
-                scale = jnp.where(meta_ref[2 * slot] == row, jnp.exp(max_ref[slot] - peak), 0.0)
-                total = total + scale * total_ref[slot]
-                summed = summed + scale * sum_ref[slot]
+                slot_max, slot_total, slot_sum = of_slot(slot)
+                scale = jnp.where(meta_ref[2 * slot] == row, jnp.exp(slot_max - peak), 0.0)
+                total = total + scale * slot_total
+                summed = summed + scale * slot_sum
             stats = jnp.where(lanes < TOTAL_LANE, peak, total)
             for part in range(heads // per):
                 dest = row * (heads // per) + part
@@ -227,38 +243,58 @@
     out_one, out_three = gathered(1, 3)
     got_one = shifted(out_one, side, 1, 0)
     got_three = shifted(out_three, side, 3, 0)
-    queries, got_two = lax.optimization_barrier((queries, got_two))
+    queries, out_one = lax.optimization_barrier((queries, out_one))
 
     group = 4
+    start = 20 // group * group
+    whole = pl.BlockSpec((rows, heads, width), lambda i, *_: (0, 0, 0))
+    partial = [jax.ShapeDtypeStruct((start, heads, width), jnp.float32)] * 3
+    partial_specs = [pl.BlockSpec((start, heads, width), lambda i, *_: (0, 0, 0))] * 3
+    params = pltpu.CompilerParams(dimension_semantics=("arbitrary",), vmem_limit_bytes=8 * 1024 * 1024)
+    meta = slot_meta.reshape(-1)
+    early = pl.pallas_call(
+        functools.partial(attend_early, group),
+        out_shape=partial,
+        grid_spec=pltpu.PrefetchScalarGridSpec(
+            num_scalar_prefetch=2,
+            grid=(start // group,),
+            in_specs=[whole, pl.BlockSpec((group,) + kv_cache.shape[1:], lambda i, *_: (i, 0, 0, 0, 0))],
+            out_specs=partial_specs,
+        ),
+        compiler_params=params,
+        cost_estimate=BRIEF,
+        name="attend_early",
+    )(meta, row_len, queries, kv_cache)
+    early, got_two = lax.optimization_barrier((early, got_two))
     parts = pl.pallas_call(
-        functools.partial(attend_kernel, slots, group),
+        functools.partial(attend_late, slots, start, group),
         out_shape=jax.ShapeDtypeStruct((pairs, 2 * per, width), jnp.float32),
         grid_spec=pltpu.PrefetchScalarGridSpec(
             num_scalar_prefetch=3,
-            grid=(slots // group,),
+            grid=((slots - start) // group,),
             in_specs=[
-                pl.BlockSpec((rows, heads, width), lambda i, *_: (0, 0, 0)),
-                pl.BlockSpec((group,) + kv_cache.shape[1:], lambda i, *_: (i, 0, 0, 0, 0)),
-            ],
+                whole,
+                pl.BlockSpec((group,) + kv_cache.shape[1:], lambda i, *_: (i + start // group, 0, 0, 0, 0)),
+            ]
+            + partial_specs,
             out_specs=pl.BlockSpec((pairs, 2 * per, width), lambda i, *_: (0, 0, 0)),
-            scratch_shapes=[pltpu.VMEM((slots, heads, width), jnp.float32)] * 3,
+            scratch_shapes=[pltpu.VMEM((slots - start, heads, width), jnp.float32)] * 3,
         ),
-        compiler_params=pltpu.CompilerParams(
-            dimension_semantics=("arbitrary",), vmem_limit_bytes=8 * 1024 * 1024
-        ),
+        compiler_params=params,
         cost_estimate=BRIEF,
-        name="attend",
-    )(slot_meta.reshape(-1), row_len, new_slot, queries, kv_cache)
+        name="attend_late",
+    )(meta, row_len, new_slot, queries, kv_cache, *early)
     got_two, parts = lax.optimization_barrier((got_two, parts))
     plan = functools.partial(stage_plan, turns, side, slots)
     out_early = move(plan, 6, [new_slot], [kv_cache, got_two], [2] * 3, "stage", scratch=[order])
     got_early = [shifted(array, side, turn, 1) for array, turn in zip(out_early, turns)]
     mine = lax.all_to_all(parts, "inst", split_axis=0, concat_axis=0, tiled=True)
-    out_late = move(functools.partial(split_plan, turns), 6, [], [got_one, got_three], [2] * 3, "split")
+    got_one, got_three, out_early = lax.optimization_barrier((got_one, got_three, out_early))
+    plan = functools.partial(split_plan, ((2, (0, 1)), (1, (0,)), (3, (0,)), (1, (1,)), (3, (1,))))
+    out_late = move(plan, 6, [], [got_one, got_three], [2, 1, 1, 1, 1], "split")
     got_late = [shifted(out_late[0], side, 2, 1)]
     out_late, got_early = lax.optimization_barrier((out_late, got_early))
-    got_late += [shifted(array, side, turn, 1) for array, turn in zip(out_late[1:], turns[1:])]
-
+    got_late += [shifted(array, side, turn, 1) for array, turn in zip(out_late[1:3], turns[1:])]
     details = mine[:, per, META_LANE : META_LANE + 5].astype(jnp.int32)
     where = details[:, 0]
     placing = where[None, :] == jnp.arange(pairs, dtype=jnp.int32)[:, None]
@@ -269,6 +305,9 @@
     pieces += [(4 + n, m, first, turn) for n, turn in enumerate(turns) for m, first in enumerate((0, 2))]
     moved_cache = placed([kv_cache, got_two, got_one, got_three] + got_early, pieces)
 
+    out_last, got_late[0], moved_cache = lax.optimization_barrier((out_late[3:], got_late[0], moved_cache))
+    got_last = [shifted(array, side, turn, 1) for array, turn in zip(out_last, turns[1:])]
+
     peaks = mine[:, per:, MAX_LANE : MAX_LANE + 1]
     totals = mine[:, per:, TOTAL_LANE : TOTAL_LANE + 1]
     scale = jnp.exp(peaks - peaks.max(0, keepdims=True))
@@ -276,11 +315,10 @@
     everyone = jnp.broadcast_to(done[None], (pairs,) + done.shape)
     result = lax.all_to_all(everyone, "inst", split_axis=0, concat_axis=0, tiled=True)
     result = result.reshape(1, rows, heads, width)
-    moved_cache = placed(got_late[:1], [(0, m, first, 2) for m, first in enumerate((1, 3))], moved_cache)
-    pieces = [(n, m, first, turn) for n, turn in enumerate(turns[1:]) for m, first in enumerate((1, 3))]
-    moved_cache = placed(got_late[1:], pieces, moved_cache)
-    result, moved_cache = lax.optimization_barrier((result, moved_cache))
+    pieces = [(0, 0, 1, 2), (0, 1, 3, 2), (1, 0, 1, 1), (2, 0, 1, 3)]
+    moved_cache = placed(got_late, pieces, moved_cache)
     attended = jnp.where((master == me)[None, :, None, None], result, jnp.float32(0.0))
+    moved_cache = placed(got_last, [(0, 0, 3, 1), (1, 0, 3, 3)], moved_cache)
     return (moved_cache, moved_meta, attended)
 
 

time: 105 us -> 104 us (level)
  waiting for transfers between devices: 38.9 us -> 31.6 us
  starting transfers between devices: 25.8 us -> 30.4 us
  Pallas kernels: 35.6 us -> 36.8 us
    all_to_all x1, waiting for transfers between devices: 17.4 us -> 0.01 us  [local(): lax.all_to_all(parts, 'inst', split_axis=0, concat_axis=0, tiled=True)]
    ppermute x9 -> x11, waiting for transfers between devices: 21.3 us -> 31.6 us  [shifted(): return lax.ppermute(value, ('inst', 'tp'), pairs)]
    all_to_all x1, starting transfers between devices: 4.53 us -> 6.8 us  [local(): lax.all_to_all(parts, 'inst', split_axis=0, concat_axis=0, tiled=True)]
    pallas_call x1 -> x2, Pallas kernels: 12.3 us -> 14.2 us  [the longest x1 7.55 us: local(): pl.pallas_call(functools.partial(attend_early, group), out_shape=partial,...]
    ppermute x9 -> x11, starting transfers between devices: 17.6 us -> 19.2 us  [shifted(): return lax.ppermute(value, ('inst', 'tp'), pairs)]
  transfers between devices with their start and end apart: 11 -> 13, of which waited for: 5 -> 10; matrix products, arithmetic and copies ran while one was open for 3% -> 3% of each run, Pallas kernels for 31% -> 31%
where the time goes in v4:
time: 104 us; the launch traced here: 103 us
  Pallas kernels  36.8 us (35%)
  waiting for transfers between devices  31.6 us (30%)
  starting transfers between devices  30.4 us (29%)
  local copies, waits for them, and re-layouts  1.93 us (2%)
  other arithmetic  1.45 us (1%)
    ppermute x11, waiting for transfers between devices, shifted(): return lax.ppermute(value, ('inst', 'tp'), pairs)  31.6 us
    pallas_call x7, Pallas kernels, move(): pl.pallas_call(functools.partial(move_kernel, plan, len(scalars), len(ope...  22.6 us
    ppermute x11, starting transfers between devices, shifted(): return lax.ppermute(value, ('inst', 'tp'), pairs)  19.2 us
    pallas_call x1, Pallas kernels, local(): pl.pallas_call(functools.partial(attend_early, group), out_shape=partial,...  7.55 us
    all_to_all x1, starting transfers between devices, local(): lax.all_to_all(parts, 'inst', split_axis=0, concat_axis=0, tiled=True)  6.8 us
    pallas_call x1, Pallas kernels, local(): pl.pallas_call(functools.partial(attend_late, slots, start, group), out_s...  6.65 us
    all_to_all x1, starting transfers between devices, local(): lax.all_to_all(everyone, 'inst', split_axis=0, concat_axis=0, tiled=True)  4.48 us
  transfers between devices with their start and end apart: 13, of which 10 were waited for; matrix products, arithmetic and copies ran while one was open for 3% of the time, Pallas kernels for 31%

profile of v4, /device:TPU:1, one launch (start us, length us, event | category | flops | bytes accessed | tf_op | source)
XLA Modules:
  0.0 103.0 jit_solution(16935229115487171134)
XLA Ops:
  0.6 3.2 %gather.3 = bf16[8,2,1,512,128]{4,3,2,1,0:T(8,128)(2,1)} custom-call(s32[32]{0:T(128)} %refs_0_.6, bf16[32,2,1,512,128]{4,3,2,1,0:T(8,128)(2,1)} %refs_0_.7), custom_call_target="tpu_custom_call" | custom-call | flops 1 | bytes 1 | tf_op jit(solution)/shard_map/gather/pallas_call | solution.py:118
  3.9 3.8 %collective-permute-start.2 = (bf16[8,2,1,512,128]{4,3,2,1,0:T(8,128)(2,1)}, bf16[8,2,1,512,128]{4,3,2,1,0:T(8,128)(2,1)}, u32[]{:S(2)}, u32[]{:S(2)}) collective-permute-start(bf16[8,2,1,512,128]{4,3,2,1,0:T(8,128)(2,1)} %gather.3), channel_id=1, source_target_pairs={{0,16},{1,65},{2,18},{3,67},{4,20},{5,69},{6,22},{7,71},{8,24},{9,... | collective-permute-start | bytes 6291464 | tf_op jit(solution)/shard_map/ppermute | solution.py:144
  7.7 4.3 %gather.2 = (bf16[8,2,1,512,128]{4,3,2,1,0:T(8,128)(2,1)}, bf16[8,2,1,512,128]{4,3,2,1,0:T(8,128)(2,1)}) custom-call(s32[32]{0:T(128)} %refs_0_.6, bf16[32,2,1,512,128]{4,3,2,1,0:T(8,128)(2,1)} %refs_0_.7), custom_call_target="tpu_custom_call" | custom-call | flops 1 | bytes 1 | tf_op jit(solution)/shard_map/gather/pallas_call | solution.py:118
  12.0 0.8 collective-permute-start.1
  12.8 0.7 collective-permute-start
  13.7 7.5 %attend_early.1 = (f32[20,16,128]{2,1,0:T(8,128)S(1)}, f32[20,16,128]{2,1,0:T(8,128)S(1)}, f32[20,16,128]{2,1,0:T(8,128)S(1)}) custom-call(s32[64]{0:T(128)S(1)} %reshape.72.meta_ref, s32[4]{0:T(128)S(1)} %copy-done.1, bf16[4,16,128]{2,1,0:T(8,128)(2,1)S(1)} %copy-done, bf16[32,2,1,512,128]{4,3,2,1,0:T(8,128)(2,1)} %refs_0_.7), custom_call_target="tpu_custom_call" | custom-call | flops 1 | bytes 1 | tf_op jit(solution)/shard_map/attend_early/pallas_call | solution.py:255
  21.3 10.5 %collective-permute-done.2.refs_2_.refs_1_ = bf16[8,2,1,512,128]{4,3,2,1,0:T(8,128)(2,1)} collective-permute-done((bf16[8,2,1,512,128]{4,3,2,1,0:T(8,128)(2,1)}, bf16[8,2,1,512,128]{4,3,2,1,0:T(8,128)(2,1)}, u32[]{:S(2)}, u32[]{:S(2)}) %collective-permute-start.2) | collective-permute-done | bytes 2097184 | tf_op jit(solution)/shard_map/ppermute | solution.py:144
  31.8 6.6 %attend_late.1 = f32[16,8,128]{2,1,0:T(8,128)} custom-call(s32[64]{0:T(128)S(1)} %reshape.72.meta_ref, s32[4]{0:T(128)S(1)} %copy-done.1, s32[32]{0:T(128)} %refs_0_.6, bf16[4,16,128]{2,1,0:T(8,128)(2,1)S(1)} %copy-done, bf16[32,2,1,512,128]{4,3,2,1,0:T(8,128)(2,1)} %refs_0_.7, f32[20,16,128]{2,1,0:T(8,128)S(1)} %get-tuple-element.43.refs_0_, ...), custom_call_target="tpu_custom_call" | custom-call | flops 1 | bytes 1 | tf_op jit(solution)/shard_map/attend_late/pallas_call | solution.py:269
  38.4 6.8 %all-to-all-start = ((f32[16,8,128]{2,1,0:T(8,128)}), f32[16,8,128]{2,1,0:T(8,128)S(1)}, u32[]{:S(2)}, u32[]{:S(2)}) async-start(f32[16,8,128]{2,1,0:T(8,128)} %attend_late.1), calls=%async_computation | async-start | bytes 131072 | tf_op jit(solution)/shard_map/all_to_all | solution.py:291
  45.2 3.6 %stage.1 = (bf16[4,2,1,512,128]{4,3,2,1,0:T(8,128)(2,1)}, bf16[4,2,1,512,128]{4,3,2,1,0:T(8,128)(2,1)}, bf16[4,2,1,512,128]{4,3,2,1,0:T(8,128)(2,1)}) custom-call(s32[32]{0:T(128)} %refs_0_.6, bf16[32,2,1,512,128]{4,3,2,1,0:T(8,128)(2,1)} %refs_0_.7, bf16[8,2,1,512,128]{4,3,2,1,0:T(8,128)(2,1)} %collective-permute-done.2.refs_2_.refs_1_), custom_call_target="tpu_custom_call" | custom-call | flops 1 | bytes 1 | tf_op jit(solution)/shard_map/stage/pallas_call | solution.py:118
  48.8 2.9 %collective-permute-start.3 = (bf16[4,2,1,512,128]{4,3,2,1,0:T(8,128)(2,1)}, bf16[4,2,1,512,128]{4,3,2,1,0:T(8,128)(2,1)S(1)}, u32[]{:S(2)}, u32[]{:S(2)}) collective-permute-start(bf16[4,2,1,512,128]{4,3,2,1,0:T(8,128)(2,1)} %get-tuple-element.47), channel_id=1, source_target_pairs={{0,64},{1,17},{2,66},{3,19},{4,68},{5,21},{6,70},{7,23},{8,72},{9,... | collective-permute-start | bytes 3145736 | tf_op jit(solution)/shard_map/ppermute | solution.py:144
  51.8 0.3 collective-permute-start.4
  52.1 2.4 %collective-permute-start.5 = (bf16[4,2,1,512,128]{4,3,2,1,0:T(8,128)(2,1)}, bf16[4,2,1,512,128]{4,3,2,1,0:T(8,128)(2,1)}, u32[]{:S(2)}, u32[]{:S(2)}) collective-permute-start(bf16[4,2,1,512,128]{4,3,2,1,0:T(8,128)(2,1)} %get-tuple-element.49), channel_id=1, source_target_pairs={{0,96},{1,25},{2,98},{3,27},{4,100},{5,29},{6,102},{7,31},{8,104},... | collective-permute-start | bytes 3145736 | tf_op jit(solution)/shard_map/ppermute | solution.py:144
  54.5 0.5 collective-permute-done.1.refs_1_.refs_3_
  55.0 2.9 %split.1 = (bf16[4,2,1,512,128]{4,3,2,1,0:T(8,128)(2,1)}, bf16[2,2,1,512,128]{4,3,2,1,0:T(8,128)(2,1)}, bf16[2,2,1,512,128]{4,3,2,1,0:T(8,128)(2,1)}, bf16[2,2,1...) custom-call(bf16[8,2,1,512,128]{4,3,2,1,0:T(8,128)(2,1)} %collective-permute-done.refs_0_.refs_2_, ...), custom_call_target="tpu_custom_call" | custom-call | flops 1 | bytes 1 | tf_op jit(solution)/shard_map/split/pallas_call | solution.py:118
  57.9 2.8 %collective-permute-start.6 = (bf16[4,2,1,512,128]{4,3,2,1,0:T(8,128)(2,1)}, bf16[4,2,1,512,128]{4,3,2,1,0:T(8,128)(2,1)}, u32[]{:S(2)}, u32[]{:S(2)}) collective-permute-start(bf16[4,2,1,512,128]{4,3,2,1,0:T(8,128)(2,1)} %get-tuple-element.52), channel_id=1, source_target_pairs={{0,64},{1,17},{2,66},{3,19},{4,68},{5,21},{6,70},{7,23},{8,72},{9,... | collective-permute-start | bytes 3145736 | tf_op jit(solution)/shard_map/ppermute | solution.py:144
  61.6 0.6 broadcast_in_dim.47
  62.2 4.5 %all-to-all-start.1 = ((f32[16,4,128]{2,1,0:T(4,128)}), f32[16,4,128]{2,1,0:T(4,128)S(1)}, u32[]{:S(2)}, u32[]{:S(2)}) async-start(f32[16,4,128]{2,1,0:T(4,128)} %broadcast_in_dim.47), calls=%async_computation.1 | async-start | bytes 65536 | tf_op jit(solution)/shard_map/all_to_all | solution.py:316
  66.7 0.4 collective-permute-done.3.refs_4_
  67.1 11.3 %collective-permute-done.4.refs_5_ = bf16[4,2,1,512,128]{4,3,2,1,0:T(8,128)(2,1)} collective-permute-done((bf16[4,2,1,512,128]{4,3,2,1,0:T(8,128)(2,1)}, bf16[4,2,1,512,128]{4,3,2,1,0:T(8,128)(2,1)}, u32[]{:S(2)}, u32[]{:S(2)}) %collective-permute-start.4) | collective-permute-done | bytes 1048608 | tf_op jit(solution)/shard_map/ppermute | solution.py:144
  78.7 1.2 %collective-permute-start.9 = (bf16[2,2,1,512,128]{4,3,2,1,0:T(8,128)(2,1)}, bf16[2,2,1,512,128]{4,3,2,1,0:T(8,128)(2,1)}, u32[]{:S(2)}, u32[]{:S(2)}) collective-permute-start(bf16[2,2,1,512,128]{4,3,2,1,0:T(8,128)(2,1)} %get-tuple-element.66), channel_id=1, source_target_pairs={{0,32},{1,9},{2,34},{3,11},{4,36},{5,13},{6,38},{7,15},{8,40},{9,1... | collective-permute-start | bytes 1572872 | tf_op jit(solution)/shard_map/ppermute | solution.py:144
  79.8 1.5 %collective-permute-start.10 = (bf16[2,2,1,512,128]{4,3,2,1,0:T(8,128)(2,1)}, bf16[2,2,1,512,128]{4,3,2,1,0:T(8,128)(2,1)}, u32[]{:S(2)}, u32[]{:S(2)}) collective-permute-start(bf16[2,2,1,512,128]{4,3,2,1,0:T(8,128)(2,1)} %get-tuple-element.67), channel_id=1, source_target_pairs={{0,96},{1,25},{2,98},{3,27},{4,100},{5,29},{6,102},{7,31},{8,104},... | collective-permute-start | bytes 1572872 | tf_op jit(solution)/shard_map/ppermute | solution.py:144
  81.3 4.6 %place.3.refs_4_ = bf16[32,2,1,512,128]{4,3,2,1,0:T(8,128)(2,1)} custom-call(bf16[32,2,1,512,128]{4,3,2,1,0:T(8,128)(2,1)} %refs_0_.7, bf16[8,2,1,512,128]{4,3,2,1,0:T(8,128)(2,1)} %collective-permute-done.2.refs_2_.refs_1_, bf16[8,2,1,512,128]{4,3,2,1,0:T(8,128)(2,1)} %collective-permute-done.refs_0_.refs_2_, ...), custom_call_target="tpu_custom_call" | custom-call | flops 1 | bytes 1 | tf_op jit(solution)/shard_map/place/pallas_call | solution.py:118
  86.0 4.0 %collective-permute-done.6.refs_0_ = bf16[4,2,1,512,128]{4,3,2,1,0:T(8,128)(2,1)} collective-permute-done((bf16[4,2,1,512,128]{4,3,2,1,0:T(8,128)(2,1)}, bf16[4,2,1,512,128]{4,3,2,1,0:T(8,128)(2,1)}, u32[]{:S(2)}, u32[]{:S(2)}) %collective-permute-start.6) | collective-permute-done | bytes 1048608 | tf_op jit(solution)/shard_map/ppermute | solution.py:144
  90.0 1.3 %collective-permute-start.7 = (bf16[2,2,1,512,128]{4,3,2,1,0:T(8,128)(2,1)}, bf16[2,2,1,512,128]{4,3,2,1,0:T(8,128)(2,1)S(1)}, u32[]{:S(2)}, u32[]{:S(2)}) collective-permute-start(bf16[2,2,1,512,128]{4,3,2,1,0:T(8,128)(2,1)} %get-tuple-element.63), channel_id=1, source_target_pairs={{0,32},{1,9},{2,34},{3,11},{4,36},{5,13},{6,38},{7,15},{8,40},{9,1... | collective-permute-start | bytes 1572872 | tf_op jit(solution)/shard_map/ppermute | solution.py:144
  91.3 1.4 %collective-permute-start.8 = (bf16[2,2,1,512,128]{4,3,2,1,0:T(8,128)(2,1)}, bf16[2,2,1,512,128]{4,3,2,1,0:T(8,128)(2,1)S(1)}, u32[]{:S(2)}, u32[]{:S(2)}) collective-permute-start(bf16[2,2,1,512,128]{4,3,2,1,0:T(8,128)(2,1)} %get-tuple-element.64), channel_id=1, source_target_pairs={{0,96},{1,25},{2,98},{3,27},{4,100},{5,29},{6,102},{7,31},{8,104},... | collective-permute-start | bytes 1572872 | tf_op jit(solution)/shard_map/ppermute | solution.py:144
  92.9 0.6 copy.35
  93.6 0.7 broadcast_select_fusion
  94.3 1.4 %collective-permute-done.9.refs_1_ = bf16[2,2,1,512,128]{4,3,2,1,0:T(8,128)(2,1)} collective-permute-done((bf16[2,2,1,512,128]{4,3,2,1,0:T(8,128)(2,1)}, bf16[2,2,1,512,128]{4,3,2,1,0:T(8,128)(2,1)}, u32[]{:S(2)}, u32[]{:S(2)}) %collective-permute-start.9) | collective-permute-done | bytes 524320 | tf_op jit(solution)/shard_map/ppermute | solution.py:144
  95.9 2.4 %place.4.refs_3_ = bf16[32,2,1,512,128]{4,3,2,1,0:T(8,128)(2,1)} custom-call(bf16[4,2,1,512,128]{4,3,2,1,0:T(8,128)(2,1)} %collective-permute-done.6.refs_0_, bf16[2,2,1,512,128]{4,3,2,1,0:T(8,128)(2,1)} %collective-permute-done.9.refs_1_, bf16[2,2,1,512,128]{4,3,2,1,0:T(8,128)(2,1)} %collective-permute-done.10.refs_2_, ...), custom_call_target="tpu_custom_call", output_to_operand_aliasing={{}: (4, {})} | custom-call | flops 1 | bytes 1 | tf_op jit(solution)/shard_map/place/pallas_call | solution.py:118
  98.4 2.8 %collective-permute-done.7.refs_0_ = bf16[2,2,1,512,128]{4,3,2,1,0:T(8,128)(2,1)S(1)} collective-permute-done((bf16[2,2,1,512,128]{4,3,2,1,0:T(8,128)(2,1)}, bf16[2,2,1,512,128]{4,3,2,1,0:T(8,128)(2,1)S(1)}, u32[]{:S(2)}, u32[]{:S(2)}) %collective-permute-start.7) | collective-permute-done | bytes 524320 | tf_op jit(solution)/shard_map/ppermute | solution.py:144
  101.4 1.6 %place.5 = bf16[32,2,1,512,128]{4,3,2,1,0:T(8,128)(2,1)} custom-call(bf16[2,2,1,512,128]{4,3,2,1,0:T(8,128)(2,1)S(1)} %collective-permute-done.7.refs_0_, bf16[2,2,1,512,128]{4,3,2,1,0:T(8,128)(2,1)S(1)} %collective-permute-done.8.refs_1_, s32[16]{0:T(128)S(1)} %slice_bitcast_fusion.refs_7_.refs_3_.refs_2_, ...), custom_call_target="tpu_custom_call", output_to_operand_aliasing={{}: (3, {})} | custom-call | flops 1 | bytes 1 | tf_op jit(solution)/shard_map/place/pallas_call | solution.py:118
  (31 shorter events, 2.1 us)
Async XLA Ops:
  3.8 9.7 %copy-start.2 = (s32[32,2]{0,1:T(2,128)S(1)}, s32[32,2]{0,1:T(2,128)}, u32[]{:S(2)}) copy-start(s32[32,2]{0,1:T(2,128)} %param.8) | copy-start | bytes 772
  3.8 9.9 %copy-start = (bf16[4,16,128]{2,1,0:T(8,128)(2,1)S(1)}, bf16[4,16,128]{2,1,0:T(8,128)(2,1)}, u32[]{:S(2)}) copy-start(bf16[4,16,128]{2,1,0:T(8,128)(2,1)} %q_ref.1) | copy-start | bytes 49156
  3.8 9.9 %copy-start.1 = (s32[4]{0:T(128)S(1)}, s32[4]{0:T(128)}, u32[]{:S(2)}) copy-start(s32[4]{0:T(128)} %len_ref.3) | copy-start | bytes 52
  3.9 27.9 %collective-permute-start.2 = (bf16[8,2,1,512,128]{4,3,2,1,0:T(8,128)(2,1)}, bf16[8,2,1,512,128]{4,3,2,1,0:T(8,128)(2,1)}, u32[]{:S(2)}, u32[]{:S(2)}) collective-permute-start(bf16[8,2,1,512,128]{4,3,2,1,0:T(8,128)(2,1)} %gather.3), channel_id=1, source_target_pairs={{0,16},{1,65},{2,18},{3,67},{4,20},{5,69},{6,22},{7,71},{8,24},{9,... | collective-permute-start | bytes 6291464 | tf_op jit(solution)/shard_map/ppermute | solution.py:144
  12.0 43.0 %collective-permute-start.1 = (bf16[8,2,1,512,128]{4,3,2,1,0:T(8,128)(2,1)}, bf16[8,2,1,512,128]{4,3,2,1,0:T(8,128)(2,1)S(1)}, u32[]{:S(2)}, u32[]{:S(2)}) collective-permute-start(bf16[8,2,1,512,128]{4,3,2,1,0:T(8,128)(2,1)} %get-tuple-element.37), channel_id=1, source_target_pairs={{0,24},{1,97},{2,26},{3,99},{4,28},{5,101},{6,30},{7,103},{8,0},{9... | collective-permute-start | bytes 6291464 | tf_op jit(solution)/shard_map/ppermute | solution.py:144
  12.8 42.1 %collective-permute-start = (bf16[8,2,1,512,128]{4,3,2,1,0:T(8,128)(2,1)}, bf16[8,2,1,512,128]{4,3,2,1,0:T(8,128)(2,1)}, u32[]{:S(2)}, u32[]{:S(2)}) collective-permute-start(bf16[8,2,1,512,128]{4,3,2,1,0:T(8,128)(2,1)} %get-tuple-element.36), channel_id=1, source_target_pairs={{0,8},{1,33},{2,10},{3,35},{4,12},{5,37},{6,14},{7,39},{8,16},{9,4... | collective-permute-start | bytes 6291464 | tf_op jit(solution)/shard_map/ppermute | solution.py:144
  31.8 13.5 %copy-start.3 = (s32[4]{0:T(128)S(1)}, s32[4]{0:T(128)}, u32[]{:S(2)}) copy-start(s32[4]{0:T(128)} %param.11) | copy-start | bytes 52
  38.4 22.3 %all-to-all-start = ((f32[16,8,128]{2,1,0:T(8,128)}), f32[16,8,128]{2,1,0:T(8,128)S(1)}, u32[]{:S(2)}, u32[]{:S(2)}) async-start(f32[16,8,128]{2,1,0:T(8,128)} %attend_late.1), calls=%async_computation | async-start | bytes 131072 | tf_op jit(solution)/shard_map/all_to_all | solution.py:291
  48.8 18.3 %collective-permute-start.3 = (bf16[4,2,1,512,128]{4,3,2,1,0:T(8,128)(2,1)}, bf16[4,2,1,512,128]{4,3,2,1,0:T(8,128)(2,1)S(1)}, u32[]{:S(2)}, u32[]{:S(2)}) collective-permute-start(bf16[4,2,1,512,128]{4,3,2,1,0:T(8,128)(2,1)} %get-tuple-element.47), channel_id=1, source_target_pairs={{0,64},{1,17},{2,66},{3,19},{4,68},{5,21},{6,70},{7,23},{8,72},{9,... | collective-permute-start | bytes 3145736 | tf_op jit(solution)/shard_map/ppermute | solution.py:144
  51.8 26.7 %collective-permute-start.4 = (bf16[4,2,1,512,128]{4,3,2,1,0:T(8,128)(2,1)}, bf16[4,2,1,512,128]{4,3,2,1,0:T(8,128)(2,1)}, u32[]{:S(2)}, u32[]{:S(2)}) collective-permute-start(bf16[4,2,1,512,128]{4,3,2,1,0:T(8,128)(2,1)} %get-tuple-element.48), channel_id=1, source_target_pairs={{0,32},{1,9},{2,34},{3,11},{4,36},{5,13},{6,38},{7,15},{8,40},{9,1... | collective-permute-start | bytes 3145736 | tf_op jit(solution)/shard_map/ppermute | solution.py:144
  52.1 26.6 %collective-permute-start.5 = (bf16[4,2,1,512,128]{4,3,2,1,0:T(8,128)(2,1)}, bf16[4,2,1,512,128]{4,3,2,1,0:T(8,128)(2,1)}, u32[]{:S(2)}, u32[]{:S(2)}) collective-permute-start(bf16[4,2,1,512,128]{4,3,2,1,0:T(8,128)(2,1)} %get-tuple-element.49), channel_id=1, source_target_pairs={{0,96},{1,25},{2,98},{3,27},{4,100},{5,29},{6,102},{7,31},{8,104},... | collective-permute-start | bytes 3145736 | tf_op jit(solution)/shard_map/ppermute | solution.py:144
  57.9 32.1 %collective-permute-start.6 = (bf16[4,2,1,512,128]{4,3,2,1,0:T(8,128)(2,1)}, bf16[4,2,1,512,128]{4,3,2,1,0:T(8,128)(2,1)}, u32[]{:S(2)}, u32[]{:S(2)}) collective-permute-start(bf16[4,2,1,512,128]{4,3,2,1,0:T(8,128)(2,1)} %get-tuple-element.52), channel_id=1, source_target_pairs={{0,64},{1,17},{2,66},{3,19},{4,68},{5,21},{6,70},{7,23},{8,72},{9,... | collective-permute-start | bytes 3145736 | tf_op jit(solution)/shard_map/ppermute | solution.py:144
  62.2 31.4 %all-to-all-start.1 = ((f32[16,4,128]{2,1,0:T(4,128)}), f32[16,4,128]{2,1,0:T(4,128)S(1)}, u32[]{:S(2)}, u32[]{:S(2)}) async-start(f32[16,4,128]{2,1,0:T(4,128)} %broadcast_in_dim.47), calls=%async_computation.1 | async-start | bytes 65536 | tf_op jit(solution)/shard_map/all_to_all | solution.py:316
  78.7 17.0 %collective-permute-start.9 = (bf16[2,2,1,512,128]{4,3,2,1,0:T(8,128)(2,1)}, bf16[2,2,1,512,128]{4,3,2,1,0:T(8,128)(2,1)}, u32[]{:S(2)}, u32[]{:S(2)}) collective-permute-start(bf16[2,2,1,512,128]{4,3,2,1,0:T(8,128)(2,1)} %get-tuple-element.66), channel_id=1, source_target_pairs={{0,32},{1,9},{2,34},{3,11},{4,36},{5,13},{6,38},{7,15},{8,40},{9,1... | collective-permute-start | bytes 1572872 | tf_op jit(solution)/shard_map/ppermute | solution.py:144
  79.8 16.1 %collective-permute-start.10 = (bf16[2,2,1,512,128]{4,3,2,1,0:T(8,128)(2,1)}, bf16[2,2,1,512,128]{4,3,2,1,0:T(8,128)(2,1)}, u32[]{:S(2)}, u32[]{:S(2)}) collective-permute-start(bf16[2,2,1,512,128]{4,3,2,1,0:T(8,128)(2,1)} %get-tuple-element.67), channel_id=1, source_target_pairs={{0,96},{1,25},{2,98},{3,27},{4,100},{5,29},{6,102},{7,31},{8,104},... | collective-permute-start | bytes 1572872 | tf_op jit(solution)/shard_map/ppermute | solution.py:144
  90.0 11.2 %collective-permute-start.7 = (bf16[2,2,1,512,128]{4,3,2,1,0:T(8,128)(2,1)}, bf16[2,2,1,512,128]{4,3,2,1,0:T(8,128)(2,1)S(1)}, u32[]{:S(2)}, u32[]{:S(2)}) collective-permute-start(bf16[2,2,1,512,128]{4,3,2,1,0:T(8,128)(2,1)} %get-tuple-element.63), channel_id=1, source_target_pairs={{0,32},{1,9},{2,34},{3,11},{4,36},{5,13},{6,38},{7,15},{8,40},{9,1... | collective-permute-start | bytes 1572872 | tf_op jit(solution)/shard_map/ppermute | solution.py:144
  91.3 10.2 %collective-permute-start.8 = (bf16[2,2,1,512,128]{4,3,2,1,0:T(8,128)(2,1)}, bf16[2,2,1,512,128]{4,3,2,1,0:T(8,128)(2,1)S(1)}, u32[]{:S(2)}, u32[]{:S(2)}) collective-permute-start(bf16[2,2,1,512,128]{4,3,2,1,0:T(8,128)(2,1)} %get-tuple-element.64), channel_id=1, source_target_pairs={{0,96},{1,25},{2,98},{3,27},{4,100},{5,29},{6,102},{7,31},{8,104},... | collective-permute-start | bytes 1572872 | tf_op jit(solution)/shard_map/ppermute | solution.py:144

commit v5 on v4

--- a/solution.py
+++ b/solution.py
@@ -183,7 +183,7 @@
     def _():
         rows, heads, width = q_ref.shape
         lanes = lax.broadcasted_iota(jnp.int32, (heads, width), 1)
-        per = out_ref.shape[1] // 2
+        per = out_ref.shape[2] // width - 1
 
         def of_slot(slot):
             return [ref[slot] for ref in early] if slot < start else [ref[slot - start] for ref in late]
@@ -199,20 +199,23 @@
                 scale = jnp.where(meta_ref[2 * slot] == row, jnp.exp(slot_max - peak), 0.0)
                 total = total + scale * slot_total
                 summed = summed + scale * slot_sum
-            stats = jnp.where(lanes < TOTAL_LANE, peak, total)
+            own = lax.broadcasted_iota(jnp.int32, (heads, width), 0) % per
+            stats = jnp.where(lanes == MAX_LANE + own, peak, 0.0) + jnp.where(lanes == TOTAL_LANE + own, total, 0.0)
             for part in range(heads // per):
                 dest = row * (heads // per) + part
-                out_ref[dest, :per] = summed[part * per : (part + 1) * per]
-                out_ref[dest, per:] = stats[part * per : (part + 1) * per]
-        lanes = lax.broadcasted_iota(jnp.int32, (per, width), 1)
+                for n in range(per):
+                    at = part * per + n
+                    out_ref[dest, :, n * width : (n + 1) * width] = summed[at : at + 1]
+                out_ref[dest, :, per * width :] = stats[part * per : (part + 1) * per].sum(0, keepdims=True)
+        lanes = lax.broadcasted_iota(jnp.int32, (1, width), 1)
         for k in range(slots // 2):
             dest = new_slot_ref[2 * k] // slots
             values = [k] + [meta_ref[4 * k + n] for n in range(4)]
-            tile = out_ref[dest, per:]
+            tile = out_ref[dest, :, per * width :]
             for n, value in enumerate(values):
-                value = jnp.full((per, width), value, jnp.int32).astype(jnp.float32)
+                value = jnp.full((1, width), value, jnp.int32).astype(jnp.float32)
                 tile = jnp.where(lanes == META_LANE + n, value, tile)
-            out_ref[dest, per:] = tile
+            out_ref[dest, :, per * width :] = tile
 
 
 def local(queries, kv_cache, slot_meta, row_len, new_slot, master):
@@ -268,7 +271,7 @@
     early, got_two = lax.optimization_barrier((early, got_two))
     parts = pl.pallas_call(
         functools.partial(attend_late, slots, start, group),
-        out_shape=jax.ShapeDtypeStruct((pairs, 2 * per, width), jnp.float32),
+        out_shape=jax.ShapeDtypeStruct((pairs, 1, (per + 1) * width), jnp.float32),
         grid_spec=pltpu.PrefetchScalarGridSpec(
             num_scalar_prefetch=3,
             grid=((slots - start) // group,),
@@ -277,7 +280,7 @@
                 pl.BlockSpec((group,) + kv_cache.shape[1:], lambda i, *_: (i + start // group, 0, 0, 0, 0)),
             ]
             + partial_specs,
-            out_specs=pl.BlockSpec((pairs, 2 * per, width), lambda i, *_: (0, 0, 0)),
+            out_specs=pl.BlockSpec((pairs, 1, (per + 1) * width), lambda i, *_: (0, 0, 0)),
             scratch_shapes=[pltpu.VMEM((slots - start, heads, width), jnp.float32)] * 3,
         ),
         compiler_params=params,
@@ -295,6 +298,7 @@
     got_late = [shifted(out_late[0], side, 2, 1)]
     out_late, got_early = lax.optimization_barrier((out_late, got_early))
     got_late += [shifted(array, side, turn, 1) for array, turn in zip(out_late[1:3], turns[1:])]
+    mine = mine.reshape(pairs, per + 1, width)
     details = mine[:, per, META_LANE : META_LANE + 5].astype(jnp.int32)
     where = details[:, 0]
     placing = where[None, :] == jnp.arange(pairs, dtype=jnp.int32)[:, None]
@@ -308,8 +312,8 @@
     out_last, got_late[0], moved_cache = lax.optimization_barrier((out_late[3:], got_late[0], moved_cache))
     got_last = [shifted(array, side, turn, 1) for array, turn in zip(out_last, turns[1:])]
 
-    peaks = mine[:, per:, MAX_LANE : MAX_LANE + 1]
-    totals = mine[:, per:, TOTAL_LANE : TOTAL_LANE + 1]
+    peaks = mine[:, per, MAX_LANE : MAX_LANE + per, None]
+    totals = mine[:, per, TOTAL_LANE : TOTAL_LANE + per, None]
     scale = jnp.exp(peaks - peaks.max(0, keepdims=True))
     done = jnp.sum(mine[:, :per] * scale, axis=0) / jnp.sum(totals * scale, axis=0)
     everyone = jnp.broadcast_to(done[None], (pairs,) + done.shape)

time: 104 us -> 103 us (level)
  no operation moved by 1% of the time
where the time goes in v5:
time: 103 us
  Pallas kernels  36.8 us (36%)
  waiting for transfers between devices  31.1 us (30%)
  starting transfers between devices  30.4 us (30%)
  local copies, waits for them, and re-layouts  2.09 us (2%)
  other arithmetic  1.48 us (1%)
    ppermute x11, waiting for transfers between devices, shifted(): return lax.ppermute(value, ('inst', 'tp'), pairs)  31.1 us
    pallas_call x7, Pallas kernels, move(): pl.pallas_call(functools.partial(move_kernel, plan, len(scalars), len(ope...  22.6 us
    ppermute x11, starting transfers between devices, shifted(): return lax.ppermute(value, ('inst', 'tp'), pairs)  19.2 us
    pallas_call x1, Pallas kernels, local(): pl.pallas_call(functools.partial(attend_early, group), out_shape=partial,...  7.55 us
    all_to_all x1, starting transfers between devices, local(): lax.all_to_all(parts, 'inst', split_axis=0, concat_axis=0, tiled=True)  6.8 us
    pallas_call x1, Pallas kernels, local(): pl.pallas_call(functools.partial(attend_late, slots, start, group), out_s...  6.66 us
    all_to_all x1, starting transfers between devices, local(): lax.all_to_all(everyone, 'inst', split_axis=0, concat_axis=0, tiled=True)  4.48 us
  transfers between devices with their start and end apart: 13, of which 10 were waited for; matrix products, arithmetic and copies ran while one was open for 3% of the time, Pallas kernels for 31%

profile of v5, /device:TPU:1, one launch (start us, length us, event | category | flops | bytes accessed | tf_op | source)
XLA Modules:
  0.0 102.7 jit_solution(17411281942596660428)
XLA Ops:
  0.6 3.2 %gather.3 = bf16[8,2,1,512,128]{4,3,2,1,0:T(8,128)(2,1)} custom-call(s32[32]{0:T(128)} %refs_0_.6, bf16[32,2,1,512,128]{4,3,2,1,0:T(8,128)(2,1)} %refs_0_.7), custom_call_target="tpu_custom_call" | custom-call | flops 1 | bytes 1 | tf_op jit(solution)/shard_map/gather/pallas_call | solution.py:118
  3.9 3.8 %collective-permute-start.2 = (bf16[8,2,1,512,128]{4,3,2,1,0:T(8,128)(2,1)}, bf16[8,2,1,512,128]{4,3,2,1,0:T(8,128)(2,1)}, u32[]{:S(2)}, u32[]{:S(2)}) collective-permute-start(bf16[8,2,1,512,128]{4,3,2,1,0:T(8,128)(2,1)} %gather.3), channel_id=1, source_target_pairs={{0,16},{1,65},{2,18},{3,67},{4,20},{5,69},{6,22},{7,71},{8,24},{9,... | collective-permute-start | bytes 6291464 | tf_op jit(solution)/shard_map/ppermute | solution.py:144
  7.7 4.3 %gather.2 = (bf16[8,2,1,512,128]{4,3,2,1,0:T(8,128)(2,1)}, bf16[8,2,1,512,128]{4,3,2,1,0:T(8,128)(2,1)}) custom-call(s32[32]{0:T(128)} %refs_0_.6, bf16[32,2,1,512,128]{4,3,2,1,0:T(8,128)(2,1)} %refs_0_.7), custom_call_target="tpu_custom_call" | custom-call | flops 1 | bytes 1 | tf_op jit(solution)/shard_map/gather/pallas_call | solution.py:118
  12.0 0.8 collective-permute-start.1
  12.8 0.7 collective-permute-start
  13.7 7.5 %attend_early.1 = (f32[20,16,128]{2,1,0:T(8,128)S(1)}, f32[20,16,128]{2,1,0:T(8,128)S(1)}, f32[20,16,128]{2,1,0:T(8,128)S(1)}) custom-call(s32[64]{0:T(128)S(1)} %reshape.132.meta_ref, s32[4]{0:T(128)S(1)} %copy-done.1, bf16[4,16,128]{2,1,0:T(8,128)(2,1)S(1)} %copy-done, bf16[32,2,1,512,128]{4,3,2,1,0:T(8,128)(2,1)} %refs_0_.7), custom_call_target="tpu_custom_call" | custom-call | flops 1 | bytes 1 | tf_op jit(solution)/shard_map/attend_early/pallas_call | solution.py:258
  21.3 10.5 %collective-permute-done.2.refs_2_.refs_1_ = bf16[8,2,1,512,128]{4,3,2,1,0:T(8,128)(2,1)} collective-permute-done((bf16[8,2,1,512,128]{4,3,2,1,0:T(8,128)(2,1)}, bf16[8,2,1,512,128]{4,3,2,1,0:T(8,128)(2,1)}, u32[]{:S(2)}, u32[]{:S(2)}) %collective-permute-start.2) | collective-permute-done | bytes 2097184 | tf_op jit(solution)/shard_map/ppermute | solution.py:144
  31.8 6.7 %attend_late.1 = f32[16,1,640]{2,1,0:T(1,128)} custom-call(s32[64]{0:T(128)S(1)} %reshape.132.meta_ref, s32[4]{0:T(128)S(1)} %copy-done.1, s32[32]{0:T(128)} %refs_0_.6, bf16[4,16,128]{2,1,0:T(8,128)(2,1)S(1)} %copy-done, bf16[32,2,1,512,128]{4,3,2,1,0:T(8,128)(2,1)} %refs_0_.7, f32[20,16,128]{2,1,0:T(8,128)S(1)} %get-tuple-element.43.refs_0_, ...), custom_call_target="tpu_custom_call" | custom-call | flops 1 | bytes 1 | tf_op jit(solution)/shard_map/attend_late/pallas_call | solution.py:272
  38.4 6.8 %all-to-all-start = ((f32[16,1,640]{2,1,0:T(1,128)}), f32[16,1,640]{2,1,0:T(1,128)S(1)}, u32[]{:S(2)}, u32[]{:S(2)}) async-start(f32[16,1,640]{2,1,0:T(1,128)} %attend_late.1), calls=%async_computation | async-start | bytes 81920 | tf_op jit(solution)/shard_map/all_to_all | solution.py:294
  45.3 3.6 %stage.1 = (bf16[4,2,1,512,128]{4,3,2,1,0:T(8,128)(2,1)}, bf16[4,2,1,512,128]{4,3,2,1,0:T(8,128)(2,1)}, bf16[4,2,1,512,128]{4,3,2,1,0:T(8,128)(2,1)}) custom-call(s32[32]{0:T(128)} %refs_0_.6, bf16[32,2,1,512,128]{4,3,2,1,0:T(8,128)(2,1)} %refs_0_.7, bf16[8,2,1,512,128]{4,3,2,1,0:T(8,128)(2,1)} %collective-permute-done.2.refs_2_.refs_1_), custom_call_target="tpu_custom_call" | custom-call | flops 1 | bytes 1 | tf_op jit(solution)/shard_map/stage/pallas_call | solution.py:118
  48.9 2.9 %collective-permute-start.3 = (bf16[4,2,1,512,128]{4,3,2,1,0:T(8,128)(2,1)}, bf16[4,2,1,512,128]{4,3,2,1,0:T(8,128)(2,1)S(1)}, u32[]{:S(2)}, u32[]{:S(2)}) collective-permute-start(bf16[4,2,1,512,128]{4,3,2,1,0:T(8,128)(2,1)} %get-tuple-element.47), channel_id=1, source_target_pairs={{0,64},{1,17},{2,66},{3,19},{4,68},{5,21},{6,70},{7,23},{8,72},{9,... | collective-permute-start | bytes 3145736 | tf_op jit(solution)/shard_map/ppermute | solution.py:144
  51.8 0.3 collective-permute-start.4
  52.1 2.4 %collective-permute-start.5 = (bf16[4,2,1,512,128]{4,3,2,1,0:T(8,128)(2,1)}, bf16[4,2,1,512,128]{4,3,2,1,0:T(8,128)(2,1)}, u32[]{:S(2)}, u32[]{:S(2)}) collective-permute-start(bf16[4,2,1,512,128]{4,3,2,1,0:T(8,128)(2,1)} %get-tuple-element.49), channel_id=1, source_target_pairs={{0,96},{1,25},{2,98},{3,27},{4,100},{5,29},{6,102},{7,31},{8,104},... | collective-permute-start | bytes 3145736 | tf_op jit(solution)/shard_map/ppermute | solution.py:144
  54.5 0.3 collective-permute-done.1.refs_1_.refs_3_
  54.9 2.9 %split.1 = (bf16[4,2,1,512,128]{4,3,2,1,0:T(8,128)(2,1)}, bf16[2,2,1,512,128]{4,3,2,1,0:T(8,128)(2,1)}, bf16[2,2,1,512,128]{4,3,2,1,0:T(8,128)(2,1)}, bf16[2,2,1...) custom-call(bf16[8,2,1,512,128]{4,3,2,1,0:T(8,128)(2,1)} %collective-permute-done.refs_0_.refs_2_, ...), custom_call_target="tpu_custom_call" | custom-call | flops 1 | bytes 1 | tf_op jit(solution)/shard_map/split/pallas_call | solution.py:118
  57.8 2.8 %collective-permute-start.6 = (bf16[4,2,1,512,128]{4,3,2,1,0:T(8,128)(2,1)}, bf16[4,2,1,512,128]{4,3,2,1,0:T(8,128)(2,1)}, u32[]{:S(2)}, u32[]{:S(2)}) collective-permute-start(bf16[4,2,1,512,128]{4,3,2,1,0:T(8,128)(2,1)} %get-tuple-element.52), channel_id=1, source_target_pairs={{0,64},{1,17},{2,66},{3,19},{4,68},{5,21},{6,70},{7,23},{8,72},{9,... | collective-permute-start | bytes 3145736 | tf_op jit(solution)/shard_map/ppermute | solution.py:144
  61.7 0.6 broadcast_in_dim.47
  62.3 4.5 %all-to-all-start.1 = ((f32[16,4,128]{2,1,0:T(4,128)}), f32[16,4,128]{2,1,0:T(4,128)S(1)}, u32[]{:S(2)}, u32[]{:S(2)}) async-start(f32[16,4,128]{2,1,0:T(4,128)} %broadcast_in_dim.47), calls=%async_computation.1 | async-start | bytes 65536 | tf_op jit(solution)/shard_map/all_to_all | solution.py:320
  66.9 11.3 %collective-permute-done.4.refs_5_ = bf16[4,2,1,512,128]{4,3,2,1,0:T(8,128)(2,1)} collective-permute-done((bf16[4,2,1,512,128]{4,3,2,1,0:T(8,128)(2,1)}, bf16[4,2,1,512,128]{4,3,2,1,0:T(8,128)(2,1)}, u32[]{:S(2)}, u32[]{:S(2)}) %collective-permute-start.4) | collective-permute-done | bytes 1048608 | tf_op jit(solution)/shard_map/ppermute | solution.py:144
  78.4 1.2 %collective-permute-start.9 = (bf16[2,2,1,512,128]{4,3,2,1,0:T(8,128)(2,1)}, bf16[2,2,1,512,128]{4,3,2,1,0:T(8,128)(2,1)}, u32[]{:S(2)}, u32[]{:S(2)}) collective-permute-start(bf16[2,2,1,512,128]{4,3,2,1,0:T(8,128)(2,1)} %get-tuple-element.66), channel_id=1, source_target_pairs={{0,32},{1,9},{2,34},{3,11},{4,36},{5,13},{6,38},{7,15},{8,40},{9,1... | collective-permute-start | bytes 1572872 | tf_op jit(solution)/shard_map/ppermute | solution.py:144
  79.6 1.5 %collective-permute-start.10 = (bf16[2,2,1,512,128]{4,3,2,1,0:T(8,128)(2,1)}, bf16[2,2,1,512,128]{4,3,2,1,0:T(8,128)(2,1)}, u32[]{:S(2)}, u32[]{:S(2)}) collective-permute-start(bf16[2,2,1,512,128]{4,3,2,1,0:T(8,128)(2,1)} %get-tuple-element.67), channel_id=1, source_target_pairs={{0,96},{1,25},{2,98},{3,27},{4,100},{5,29},{6,102},{7,31},{8,104},... | collective-permute-start | bytes 1572872 | tf_op jit(solution)/shard_map/ppermute | solution.py:144
  81.1 4.6 %place.3.refs_4_ = bf16[32,2,1,512,128]{4,3,2,1,0:T(8,128)(2,1)} custom-call(bf16[32,2,1,512,128]{4,3,2,1,0:T(8,128)(2,1)} %refs_0_.7, bf16[8,2,1,512,128]{4,3,2,1,0:T(8,128)(2,1)} %collective-permute-done.2.refs_2_.refs_1_, bf16[8,2,1,512,128]{4,3,2,1,0:T(8,128)(2,1)} %collective-permute-done.refs_0_.refs_2_, ...), custom_call_target="tpu_custom_call" | custom-call | flops 1 | bytes 1 | tf_op jit(solution)/shard_map/place/pallas_call | solution.py:118
  85.7 4.0 %collective-permute-done.6.refs_0_ = bf16[4,2,1,512,128]{4,3,2,1,0:T(8,128)(2,1)} collective-permute-done((bf16[4,2,1,512,128]{4,3,2,1,0:T(8,128)(2,1)}, bf16[4,2,1,512,128]{4,3,2,1,0:T(8,128)(2,1)}, u32[]{:S(2)}, u32[]{:S(2)}) %collective-permute-start.6) | collective-permute-done | bytes 1048608 | tf_op jit(solution)/shard_map/ppermute | solution.py:144
  89.7 1.3 %collective-permute-start.7 = (bf16[2,2,1,512,128]{4,3,2,1,0:T(8,128)(2,1)}, bf16[2,2,1,512,128]{4,3,2,1,0:T(8,128)(2,1)S(1)}, u32[]{:S(2)}, u32[]{:S(2)}) collective-permute-start(bf16[2,2,1,512,128]{4,3,2,1,0:T(8,128)(2,1)} %get-tuple-element.63), channel_id=1, source_target_pairs={{0,32},{1,9},{2,34},{3,11},{4,36},{5,13},{6,38},{7,15},{8,40},{9,1... | collective-permute-start | bytes 1572872 | tf_op jit(solution)/shard_map/ppermute | solution.py:144
  91.0 1.4 %collective-permute-start.8 = (bf16[2,2,1,512,128]{4,3,2,1,0:T(8,128)(2,1)}, bf16[2,2,1,512,128]{4,3,2,1,0:T(8,128)(2,1)S(1)}, u32[]{:S(2)}, u32[]{:S(2)}) collective-permute-start(bf16[2,2,1,512,128]{4,3,2,1,0:T(8,128)(2,1)} %get-tuple-element.64), channel_id=1, source_target_pairs={{0,96},{1,25},{2,98},{3,27},{4,100},{5,29},{6,102},{7,31},{8,104},... | collective-permute-start | bytes 1572872 | tf_op jit(solution)/shard_map/ppermute | solution.py:144
  92.7 0.6 copy.41
  93.3 0.7 broadcast_select_fusion
  94.0 1.4 %collective-permute-done.9.refs_1_ = bf16[2,2,1,512,128]{4,3,2,1,0:T(8,128)(2,1)} collective-permute-done((bf16[2,2,1,512,128]{4,3,2,1,0:T(8,128)(2,1)}, bf16[2,2,1,512,128]{4,3,2,1,0:T(8,128)(2,1)}, u32[]{:S(2)}, u32[]{:S(2)}) %collective-permute-start.9) | collective-permute-done | bytes 524320 | tf_op jit(solution)/shard_map/ppermute | solution.py:144
  95.7 2.4 %place.4.refs_3_ = bf16[32,2,1,512,128]{4,3,2,1,0:T(8,128)(2,1)} custom-call(bf16[4,2,1,512,128]{4,3,2,1,0:T(8,128)(2,1)} %collective-permute-done.6.refs_0_, bf16[2,2,1,512,128]{4,3,2,1,0:T(8,128)(2,1)} %collective-permute-done.9.refs_1_, bf16[2,2,1,512,128]{4,3,2,1,0:T(8,128)(2,1)} %collective-permute-done.10.refs_2_, ...), custom_call_target="tpu_custom_call", output_to_operand_aliasing={{}: (4, {})} | custom-call | flops 1 | bytes 1 | tf_op jit(solution)/shard_map/place/pallas_call | solution.py:118
  98.1 2.8 %collective-permute-done.7.refs_0_ = bf16[2,2,1,512,128]{4,3,2,1,0:T(8,128)(2,1)S(1)} collective-permute-done((bf16[2,2,1,512,128]{4,3,2,1,0:T(8,128)(2,1)}, bf16[2,2,1,512,128]{4,3,2,1,0:T(8,128)(2,1)S(1)}, u32[]{:S(2)}, u32[]{:S(2)}) %collective-permute-start.7) | collective-permute-done | bytes 524320 | tf_op jit(solution)/shard_map/ppermute | solution.py:144
  100.9 0.3 collective-permute-done.8.refs_1_
  101.2 1.6 %place.5 = bf16[32,2,1,512,128]{4,3,2,1,0:T(8,128)(2,1)} custom-call(bf16[2,2,1,512,128]{4,3,2,1,0:T(8,128)(2,1)S(1)} %collective-permute-done.7.refs_0_, bf16[2,2,1,512,128]{4,3,2,1,0:T(8,128)(2,1)S(1)} %collective-permute-done.8.refs_1_, s32[16]{0:T(128)S(1)} %slice_bitcast_fusion.refs_7_.refs_3_.refs_2_, ...), custom_call_target="tpu_custom_call", output_to_operand_aliasing={{}: (3, {})} | custom-call | flops 1 | bytes 1 | tf_op jit(solution)/shard_map/place/pallas_call | solution.py:118
  (37 shorter events, 2.2 us)
Async XLA Ops:
  3.8 9.7 %copy-start.2 = (s32[32,2]{0,1:T(2,128)S(1)}, s32[32,2]{0,1:T(2,128)}, u32[]{:S(2)}) copy-start(s32[32,2]{0,1:T(2,128)} %param.8) | copy-start | bytes 772
  3.8 9.9 %copy-start = (bf16[4,16,128]{2,1,0:T(8,128)(2,1)S(1)}, bf16[4,16,128]{2,1,0:T(8,128)(2,1)}, u32[]{:S(2)}) copy-start(bf16[4,16,128]{2,1,0:T(8,128)(2,1)} %q_ref.1) | copy-start | bytes 49156
  3.9 9.9 %copy-start.1 = (s32[4]{0:T(128)S(1)}, s32[4]{0:T(128)}, u32[]{:S(2)}) copy-start(s32[4]{0:T(128)} %len_ref.3) | copy-start | bytes 52
  3.9 27.9 %collective-permute-start.2 = (bf16[8,2,1,512,128]{4,3,2,1,0:T(8,128)(2,1)}, bf16[8,2,1,512,128]{4,3,2,1,0:T(8,128)(2,1)}, u32[]{:S(2)}, u32[]{:S(2)}) collective-permute-start(bf16[8,2,1,512,128]{4,3,2,1,0:T(8,128)(2,1)} %gather.3), channel_id=1, source_target_pairs={{0,16},{1,65},{2,18},{3,67},{4,20},{5,69},{6,22},{7,71},{8,24},{9,... | collective-permute-start | bytes 6291464 | tf_op jit(solution)/shard_map/ppermute | solution.py:144
  12.0 42.9 %collective-permute-start.1 = (bf16[8,2,1,512,128]{4,3,2,1,0:T(8,128)(2,1)}, bf16[8,2,1,512,128]{4,3,2,1,0:T(8,128)(2,1)S(1)}, u32[]{:S(2)}, u32[]{:S(2)}) collective-permute-start(bf16[8,2,1,512,128]{4,3,2,1,0:T(8,128)(2,1)} %get-tuple-element.37), channel_id=1, source_target_pairs={{0,24},{1,97},{2,26},{3,99},{4,28},{5,101},{6,30},{7,103},{8,0},{9... | collective-permute-start | bytes 6291464 | tf_op jit(solution)/shard_map/ppermute | solution.py:144
  12.8 42.0 %collective-permute-start = (bf16[8,2,1,512,128]{4,3,2,1,0:T(8,128)(2,1)}, bf16[8,2,1,512,128]{4,3,2,1,0:T(8,128)(2,1)}, u32[]{:S(2)}, u32[]{:S(2)}) collective-permute-start(bf16[8,2,1,512,128]{4,3,2,1,0:T(8,128)(2,1)} %get-tuple-element.36), channel_id=1, source_target_pairs={{0,8},{1,33},{2,10},{3,35},{4,12},{5,37},{6,14},{7,39},{8,16},{9,4... | collective-permute-start | bytes 6291464 | tf_op jit(solution)/shard_map/ppermute | solution.py:144
  31.8 13.5 %copy-start.3 = (s32[4]{0:T(128)S(1)}, s32[4]{0:T(128)}, u32[]{:S(2)}) copy-start(s32[4]{0:T(128)} %param.11) | copy-start | bytes 52
  38.4 22.1 %all-to-all-start = ((f32[16,1,640]{2,1,0:T(1,128)}), f32[16,1,640]{2,1,0:T(1,128)S(1)}, u32[]{:S(2)}, u32[]{:S(2)}) async-start(f32[16,1,640]{2,1,0:T(1,128)} %attend_late.1), calls=%async_computation | async-start | bytes 81920 | tf_op jit(solution)/shard_map/all_to_all | solution.py:294
  48.9 18.0 %collective-permute-start.3 = (bf16[4,2,1,512,128]{4,3,2,1,0:T(8,128)(2,1)}, bf16[4,2,1,512,128]{4,3,2,1,0:T(8,128)(2,1)S(1)}, u32[]{:S(2)}, u32[]{:S(2)}) collective-permute-start(bf16[4,2,1,512,128]{4,3,2,1,0:T(8,128)(2,1)} %get-tuple-element.47), channel_id=1, source_target_pairs={{0,64},{1,17},{2,66},{3,19},{4,68},{5,21},{6,70},{7,23},{8,72},{9,... | collective-permute-start | bytes 3145736 | tf_op jit(solution)/shard_map/ppermute | solution.py:144
  51.8 26.4 %collective-permute-start.4 = (bf16[4,2,1,512,128]{4,3,2,1,0:T(8,128)(2,1)}, bf16[4,2,1,512,128]{4,3,2,1,0:T(8,128)(2,1)}, u32[]{:S(2)}, u32[]{:S(2)}) collective-permute-start(bf16[4,2,1,512,128]{4,3,2,1,0:T(8,128)(2,1)} %get-tuple-element.48), channel_id=1, source_target_pairs={{0,32},{1,9},{2,34},{3,11},{4,36},{5,13},{6,38},{7,15},{8,40},{9,1... | collective-permute-start | bytes 3145736 | tf_op jit(solution)/shard_map/ppermute | solution.py:144
  52.1 26.3 %collective-permute-start.5 = (bf16[4,2,1,512,128]{4,3,2,1,0:T(8,128)(2,1)}, bf16[4,2,1,512,128]{4,3,2,1,0:T(8,128)(2,1)}, u32[]{:S(2)}, u32[]{:S(2)}) collective-permute-start(bf16[4,2,1,512,128]{4,3,2,1,0:T(8,128)(2,1)} %get-tuple-element.49), channel_id=1, source_target_pairs={{0,96},{1,25},{2,98},{3,27},{4,100},{5,29},{6,102},{7,31},{8,104},... | collective-permute-start | bytes 3145736 | tf_op jit(solution)/shard_map/ppermute | solution.py:144
  57.8 32.0 %collective-permute-start.6 = (bf16[4,2,1,512,128]{4,3,2,1,0:T(8,128)(2,1)}, bf16[4,2,1,512,128]{4,3,2,1,0:T(8,128)(2,1)}, u32[]{:S(2)}, u32[]{:S(2)}) collective-permute-start(bf16[4,2,1,512,128]{4,3,2,1,0:T(8,128)(2,1)} %get-tuple-element.52), channel_id=1, source_target_pairs={{0,64},{1,17},{2,66},{3,19},{4,68},{5,21},{6,70},{7,23},{8,72},{9,... | collective-permute-start | bytes 3145736 | tf_op jit(solution)/shard_map/ppermute | solution.py:144
  62.3 31.1 %all-to-all-start.1 = ((f32[16,4,128]{2,1,0:T(4,128)}), f32[16,4,128]{2,1,0:T(4,128)S(1)}, u32[]{:S(2)}, u32[]{:S(2)}) async-start(f32[16,4,128]{2,1,0:T(4,128)} %broadcast_in_dim.47), calls=%async_computation.1 | async-start | bytes 65536 | tf_op jit(solution)/shard_map/all_to_all | solution.py:320
  78.4 17.0 %collective-permute-start.9 = (bf16[2,2,1,512,128]{4,3,2,1,0:T(8,128)(2,1)}, bf16[2,2,1,512,128]{4,3,2,1,0:T(8,128)(2,1)}, u32[]{:S(2)}, u32[]{:S(2)}) collective-permute-start(bf16[2,2,1,512,128]{4,3,2,1,0:T(8,128)(2,1)} %get-tuple-element.66), channel_id=1, source_target_pairs={{0,32},{1,9},{2,34},{3,11},{4,36},{5,13},{6,38},{7,15},{8,40},{9,1... | collective-permute-start | bytes 1572872 | tf_op jit(solution)/shard_map/ppermute | solution.py:144
  79.6 16.1 %collective-permute-start.10 = (bf16[2,2,1,512,128]{4,3,2,1,0:T(8,128)(2,1)}, bf16[2,2,1,512,128]{4,3,2,1,0:T(8,128)(2,1)}, u32[]{:S(2)}, u32[]{:S(2)}) collective-permute-start(bf16[2,2,1,512,128]{4,3,2,1,0:T(8,128)(2,1)} %get-tuple-element.67), channel_id=1, source_target_pairs={{0,96},{1,25},{2,98},{3,27},{4,100},{5,29},{6,102},{7,31},{8,104},... | collective-permute-start | bytes 1572872 | tf_op jit(solution)/shard_map/ppermute | solution.py:144
  89.7 11.2 %collective-permute-start.7 = (bf16[2,2,1,512,128]{4,3,2,1,0:T(8,128)(2,1)}, bf16[2,2,1,512,128]{4,3,2,1,0:T(8,128)(2,1)S(1)}, u32[]{:S(2)}, u32[]{:S(2)}) collective-permute-start(bf16[2,2,1,512,128]{4,3,2,1,0:T(8,128)(2,1)} %get-tuple-element.63), channel_id=1, source_target_pairs={{0,32},{1,9},{2,34},{3,11},{4,36},{5,13},{6,38},{7,15},{8,40},{9,1... | collective-permute-start | bytes 1572872 | tf_op jit(solution)/shard_map/ppermute | solution.py:144
  91.0 10.2 %collective-permute-start.8 = (bf16[2,2,1,512,128]{4,3,2,1,0:T(8,128)(2,1)}, bf16[2,2,1,512,128]{4,3,2,1,0:T(8,128)(2,1)S(1)}, u32[]{:S(2)}, u32[]{:S(2)}) collective-permute-start(bf16[2,2,1,512,128]{4,3,2,1,0:T(8,128)(2,1)} %get-tuple-element.64), channel_id=1, source_target_pairs={{0,96},{1,25},{2,98},{3,27},{4,100},{5,29},{6,102},{7,31},{8,104},... | collective-permute-start | bytes 1572872 | tf_op jit(solution)/shard_map/ppermute | solution.py:144

commit v6 on v5

--- a/solution.py
+++ b/solution.py
@@ -248,8 +248,8 @@
     got_three = shifted(out_three, side, 3, 0)
     queries, out_one = lax.optimization_barrier((queries, out_one))
 
-    group = 4
-    start = 20 // group * group
+    group = 8
+    start = 16 // group * group
     whole = pl.BlockSpec((rows, heads, width), lambda i, *_: (0, 0, 0))
     partial = [jax.ShapeDtypeStruct((start, heads, width), jnp.float32)] * 3
     partial_specs = [pl.BlockSpec((start, heads, width), lambda i, *_: (0, 0, 0))] * 3

time: 103 us -> 104 us (level)
    pallas_call x1, Pallas kernels: 7.55 us -> 6.34 us  [local(): pl.pallas_call(functools.partial(attend_early, group), out_shape=partial,...]
    pallas_call x1, Pallas kernels: 6.66 us -> 7.79 us  [local(): pl.pallas_call(functools.partial(attend_late, slots, start, group), out_s...]
  transfers between devices with their start and end apart: 13 -> 13, of which waited for: 10 -> 8; matrix products, arithmetic and copies ran while one was open for 3% -> 3% of each run, Pallas kernels for 31% -> 31%
where the time goes in v6:
time: 104 us; the launch traced here: 103 us
  Pallas kernels  36.7 us (35%)
  waiting for transfers between devices  31.6 us (30%)
  starting transfers between devices  30 us (29%)
  local copies, waits for them, and re-layouts  2.09 us (2%)
  other arithmetic  1.48 us (1%)
    ppermute x11, waiting for transfers between devices, shifted(): return lax.ppermute(value, ('inst', 'tp'), pairs)  31.6 us
    pallas_call x7, Pallas kernels, move(): pl.pallas_call(functools.partial(move_kernel, plan, len(scalars), len(ope...  22.6 us
    ppermute x11, starting transfers between devices, shifted(): return lax.ppermute(value, ('inst', 'tp'), pairs)  18.4 us
    pallas_call x1, Pallas kernels, local(): pl.pallas_call(functools.partial(attend_late, slots, start, group), out_s...  7.79 us
    all_to_all x1, starting transfers between devices, local(): lax.all_to_all(parts, 'inst', split_axis=0, concat_axis=0, tiled=True)  6.8 us
    pallas_call x1, Pallas kernels, local(): pl.pallas_call(functools.partial(attend_early, group), out_shape=partial,...  6.34 us
    all_to_all x1, starting transfers between devices, local(): lax.all_to_all(everyone, 'inst', split_axis=0, concat_axis=0, tiled=True)  4.81 us
  transfers between devices with their start and end apart: 13, of which 8 were waited for; matrix products, arithmetic and copies ran while one was open for 3% of the time, Pallas kernels for 31%

profile of v6, /device:TPU:1, one launch (start us, length us, event | category | flops | bytes accessed | tf_op | source)
XLA Modules:
  0.0 102.7 jit_solution(17222033573733078524)
XLA Ops:
  0.6 3.2 %gather.3 = bf16[8,2,1,512,128]{4,3,2,1,0:T(8,128)(2,1)} custom-call(s32[32]{0:T(128)} %refs_0_.6, bf16[32,2,1,512,128]{4,3,2,1,0:T(8,128)(2,1)} %refs_0_.7), custom_call_target="tpu_custom_call" | custom-call | flops 1 | bytes 1 | tf_op jit(solution)/shard_map/gather/pallas_call | solution.py:118
  3.9 3.8 %collective-permute-start.2 = (bf16[8,2,1,512,128]{4,3,2,1,0:T(8,128)(2,1)}, bf16[8,2,1,512,128]{4,3,2,1,0:T(8,128)(2,1)}, u32[]{:S(2)}, u32[]{:S(2)}) collective-permute-start(bf16[8,2,1,512,128]{4,3,2,1,0:T(8,128)(2,1)} %gather.3), channel_id=1, source_target_pairs={{0,16},{1,65},{2,18},{3,67},{4,20},{5,69},{6,22},{7,71},{8,24},{9,... | collective-permute-start | bytes 6291464 | tf_op jit(solution)/shard_map/ppermute | solution.py:144
  7.7 4.3 %gather.2 = (bf16[8,2,1,512,128]{4,3,2,1,0:T(8,128)(2,1)}, bf16[8,2,1,512,128]{4,3,2,1,0:T(8,128)(2,1)}) custom-call(s32[32]{0:T(128)} %refs_0_.6, bf16[32,2,1,512,128]{4,3,2,1,0:T(8,128)(2,1)} %refs_0_.7), custom_call_target="tpu_custom_call" | custom-call | flops 1 | bytes 1 | tf_op jit(solution)/shard_map/gather/pallas_call | solution.py:118
  12.0 0.8 collective-permute-start.1
  12.8 0.7 collective-permute-start
  13.7 6.3 %attend_early.1 = (f32[16,16,128]{2,1,0:T(8,128)S(1)}, f32[16,16,128]{2,1,0:T(8,128)S(1)}, f32[16,16,128]{2,1,0:T(8,128)S(1)}) custom-call(s32[64]{0:T(128)S(1)} %reshape.132.meta_ref, s32[4]{0:T(128)S(1)} %copy-done.1, bf16[4,16,128]{2,1,0:T(8,128)(2,1)S(1)} %copy-done, bf16[32,2,1,512,128]{4,3,2,1,0:T(8,128)(2,1)} %refs_0_.7), custom_call_target="tpu_custom_call" | custom-call | flops 1 | bytes 1 | tf_op jit(solution)/shard_map/attend_early/pallas_call | solution.py:258
  20.1 11.7 %collective-permute-done.2.refs_2_.refs_1_ = bf16[8,2,1,512,128]{4,3,2,1,0:T(8,128)(2,1)} collective-permute-done((bf16[8,2,1,512,128]{4,3,2,1,0:T(8,128)(2,1)}, bf16[8,2,1,512,128]{4,3,2,1,0:T(8,128)(2,1)}, u32[]{:S(2)}, u32[]{:S(2)}) %collective-permute-start.2) | collective-permute-done | bytes 2097184 | tf_op jit(solution)/shard_map/ppermute | solution.py:144
  31.8 7.8 %attend_late.1 = f32[16,1,640]{2,1,0:T(1,128)} custom-call(s32[64]{0:T(128)S(1)} %reshape.132.meta_ref, s32[4]{0:T(128)S(1)} %copy-done.1, s32[32]{0:T(128)} %refs_0_.6, bf16[4,16,128]{2,1,0:T(8,128)(2,1)S(1)} %copy-done, bf16[32,2,1,512,128]{4,3,2,1,0:T(8,128)(2,1)} %refs_0_.7, f32[16,16,128]{2,1,0:T(8,128)S(1)} %get-tuple-element.43.refs_0_, ...), custom_call_target="tpu_custom_call" | custom-call | flops 1 | bytes 1 | tf_op jit(solution)/shard_map/attend_late/pallas_call | solution.py:272
  39.6 6.8 %all-to-all-start = ((f32[16,1,640]{2,1,0:T(1,128)}), f32[16,1,640]{2,1,0:T(1,128)S(1)}, u32[]{:S(2)}, u32[]{:S(2)}) async-start(f32[16,1,640]{2,1,0:T(1,128)} %attend_late.1), calls=%async_computation | async-start | bytes 81920 | tf_op jit(solution)/shard_map/all_to_all | solution.py:294
  46.4 3.6 %stage.1 = (bf16[4,2,1,512,128]{4,3,2,1,0:T(8,128)(2,1)}, bf16[4,2,1,512,128]{4,3,2,1,0:T(8,128)(2,1)}, bf16[4,2,1,512,128]{4,3,2,1,0:T(8,128)(2,1)}) custom-call(s32[32]{0:T(128)} %refs_0_.6, bf16[32,2,1,512,128]{4,3,2,1,0:T(8,128)(2,1)} %refs_0_.7, bf16[8,2,1,512,128]{4,3,2,1,0:T(8,128)(2,1)} %collective-permute-done.2.refs_2_.refs_1_), custom_call_target="tpu_custom_call" | custom-call | flops 1 | bytes 1 | tf_op jit(solution)/shard_map/stage/pallas_call | solution.py:118
  50.0 2.9 %collective-permute-start.3 = (bf16[4,2,1,512,128]{4,3,2,1,0:T(8,128)(2,1)}, bf16[4,2,1,512,128]{4,3,2,1,0:T(8,128)(2,1)S(1)}, u32[]{:S(2)}, u32[]{:S(2)}) collective-permute-start(bf16[4,2,1,512,128]{4,3,2,1,0:T(8,128)(2,1)} %get-tuple-element.47), channel_id=1, source_target_pairs={{0,64},{1,17},{2,66},{3,19},{4,68},{5,21},{6,70},{7,23},{8,72},{9,... | collective-permute-start | bytes 3145736 | tf_op jit(solution)/shard_map/ppermute | solution.py:144
  53.0 0.3 collective-permute-start.4
  53.3 2.4 %collective-permute-start.5 = (bf16[4,2,1,512,128]{4,3,2,1,0:T(8,128)(2,1)}, bf16[4,2,1,512,128]{4,3,2,1,0:T(8,128)(2,1)}, u32[]{:S(2)}, u32[]{:S(2)}) collective-permute-start(bf16[4,2,1,512,128]{4,3,2,1,0:T(8,128)(2,1)} %get-tuple-element.49), channel_id=1, source_target_pairs={{0,96},{1,25},{2,98},{3,27},{4,100},{5,29},{6,102},{7,31},{8,104},... | collective-permute-start | bytes 3145736 | tf_op jit(solution)/shard_map/ppermute | solution.py:144
  55.7 2.9 %split.1 = (bf16[4,2,1,512,128]{4,3,2,1,0:T(8,128)(2,1)}, bf16[2,2,1,512,128]{4,3,2,1,0:T(8,128)(2,1)}, bf16[2,2,1,512,128]{4,3,2,1,0:T(8,128)(2,1)}, bf16[2,2,1...) custom-call(bf16[8,2,1,512,128]{4,3,2,1,0:T(8,128)(2,1)} %collective-permute-done.refs_0_.refs_2_, ...), custom_call_target="tpu_custom_call" | custom-call | flops 1 | bytes 1 | tf_op jit(solution)/shard_map/split/pallas_call | solution.py:118
  58.5 2.0 %collective-permute-start.6 = (bf16[4,2,1,512,128]{4,3,2,1,0:T(8,128)(2,1)}, bf16[4,2,1,512,128]{4,3,2,1,0:T(8,128)(2,1)}, u32[]{:S(2)}, u32[]{:S(2)}) collective-permute-start(bf16[4,2,1,512,128]{4,3,2,1,0:T(8,128)(2,1)} %get-tuple-element.52), channel_id=1, source_target_pairs={{0,64},{1,17},{2,66},{3,19},{4,68},{5,21},{6,70},{7,23},{8,72},{9,... | collective-permute-start | bytes 3145736 | tf_op jit(solution)/shard_map/ppermute | solution.py:144
  61.7 0.6 broadcast_in_dim.47
  62.3 4.8 %all-to-all-start.1 = ((f32[16,4,128]{2,1,0:T(4,128)}), f32[16,4,128]{2,1,0:T(4,128)S(1)}, u32[]{:S(2)}, u32[]{:S(2)}) async-start(f32[16,4,128]{2,1,0:T(4,128)} %broadcast_in_dim.47), calls=%async_computation.1 | async-start | bytes 65536 | tf_op jit(solution)/shard_map/all_to_all | solution.py:320
  67.1 11.1 %collective-permute-done.4.refs_5_ = bf16[4,2,1,512,128]{4,3,2,1,0:T(8,128)(2,1)} collective-permute-done((bf16[4,2,1,512,128]{4,3,2,1,0:T(8,128)(2,1)}, bf16[4,2,1,512,128]{4,3,2,1,0:T(8,128)(2,1)}, u32[]{:S(2)}, u32[]{:S(2)}) %collective-permute-start.4) | collective-permute-done | bytes 1048608 | tf_op jit(solution)/shard_map/ppermute | solution.py:144
  78.4 1.2 %collective-permute-start.9 = (bf16[2,2,1,512,128]{4,3,2,1,0:T(8,128)(2,1)}, bf16[2,2,1,512,128]{4,3,2,1,0:T(8,128)(2,1)}, u32[]{:S(2)}, u32[]{:S(2)}) collective-permute-start(bf16[2,2,1,512,128]{4,3,2,1,0:T(8,128)(2,1)} %get-tuple-element.66), channel_id=1, source_target_pairs={{0,32},{1,9},{2,34},{3,11},{4,36},{5,13},{6,38},{7,15},{8,40},{9,1... | collective-permute-start | bytes 1572872 | tf_op jit(solution)/shard_map/ppermute | solution.py:144
  79.6 1.5 %collective-permute-start.10 = (bf16[2,2,1,512,128]{4,3,2,1,0:T(8,128)(2,1)}, bf16[2,2,1,512,128]{4,3,2,1,0:T(8,128)(2,1)}, u32[]{:S(2)}, u32[]{:S(2)}) collective-permute-start(bf16[2,2,1,512,128]{4,3,2,1,0:T(8,128)(2,1)} %get-tuple-element.67), channel_id=1, source_target_pairs={{0,96},{1,25},{2,98},{3,27},{4,100},{5,29},{6,102},{7,31},{8,104},... | collective-permute-start | bytes 1572872 | tf_op jit(solution)/shard_map/ppermute | solution.py:144
  81.1 4.6 %place.3.refs_4_ = bf16[32,2,1,512,128]{4,3,2,1,0:T(8,128)(2,1)} custom-call(bf16[32,2,1,512,128]{4,3,2,1,0:T(8,128)(2,1)} %refs_0_.7, bf16[8,2,1,512,128]{4,3,2,1,0:T(8,128)(2,1)} %collective-permute-done.2.refs_2_.refs_1_, bf16[8,2,1,512,128]{4,3,2,1,0:T(8,128)(2,1)} %collective-permute-done.refs_0_.refs_2_, ...), custom_call_target="tpu_custom_call" | custom-call | flops 1 | bytes 1 | tf_op jit(solution)/shard_map/place/pallas_call | solution.py:118
  85.7 4.0 %collective-permute-done.6.refs_0_ = bf16[4,2,1,512,128]{4,3,2,1,0:T(8,128)(2,1)} collective-permute-done((bf16[4,2,1,512,128]{4,3,2,1,0:T(8,128)(2,1)}, bf16[4,2,1,512,128]{4,3,2,1,0:T(8,128)(2,1)}, u32[]{:S(2)}, u32[]{:S(2)}) %collective-permute-start.6) | collective-permute-done | bytes 1048608 | tf_op jit(solution)/shard_map/ppermute | solution.py:144
  89.7 1.3 %collective-permute-start.7 = (bf16[2,2,1,512,128]{4,3,2,1,0:T(8,128)(2,1)}, bf16[2,2,1,512,128]{4,3,2,1,0:T(8,128)(2,1)S(1)}, u32[]{:S(2)}, u32[]{:S(2)}) collective-permute-start(bf16[2,2,1,512,128]{4,3,2,1,0:T(8,128)(2,1)} %get-tuple-element.63), channel_id=1, source_target_pairs={{0,32},{1,9},{2,34},{3,11},{4,36},{5,13},{6,38},{7,15},{8,40},{9,1... | collective-permute-start | bytes 1572872 | tf_op jit(solution)/shard_map/ppermute | solution.py:144
  91.0 1.4 %collective-permute-start.8 = (bf16[2,2,1,512,128]{4,3,2,1,0:T(8,128)(2,1)}, bf16[2,2,1,512,128]{4,3,2,1,0:T(8,128)(2,1)S(1)}, u32[]{:S(2)}, u32[]{:S(2)}) collective-permute-start(bf16[2,2,1,512,128]{4,3,2,1,0:T(8,128)(2,1)} %get-tuple-element.64), channel_id=1, source_target_pairs={{0,96},{1,25},{2,98},{3,27},{4,100},{5,29},{6,102},{7,31},{8,104},... | collective-permute-start | bytes 1572872 | tf_op jit(solution)/shard_map/ppermute | solution.py:144
  92.7 0.6 copy.41
  93.3 0.7 broadcast_select_fusion
  94.0 1.4 %collective-permute-done.9.refs_1_ = bf16[2,2,1,512,128]{4,3,2,1,0:T(8,128)(2,1)} collective-permute-done((bf16[2,2,1,512,128]{4,3,2,1,0:T(8,128)(2,1)}, bf16[2,2,1,512,128]{4,3,2,1,0:T(8,128)(2,1)}, u32[]{:S(2)}, u32[]{:S(2)}) %collective-permute-start.9) | collective-permute-done | bytes 524320 | tf_op jit(solution)/shard_map/ppermute | solution.py:144
  95.5 0.2 collective-permute-done.10.refs_2_
  95.7 2.4 %place.4.refs_3_ = bf16[32,2,1,512,128]{4,3,2,1,0:T(8,128)(2,1)} custom-call(bf16[4,2,1,512,128]{4,3,2,1,0:T(8,128)(2,1)} %collective-permute-done.6.refs_0_, bf16[2,2,1,512,128]{4,3,2,1,0:T(8,128)(2,1)} %collective-permute-done.9.refs_1_, bf16[2,2,1,512,128]{4,3,2,1,0:T(8,128)(2,1)} %collective-permute-done.10.refs_2_, ...), custom_call_target="tpu_custom_call", output_to_operand_aliasing={{}: (4, {})} | custom-call | flops 1 | bytes 1 | tf_op jit(solution)/shard_map/place/pallas_call | solution.py:118
  98.1 2.9 %collective-permute-done.7.refs_0_ = bf16[2,2,1,512,128]{4,3,2,1,0:T(8,128)(2,1)S(1)} collective-permute-done((bf16[2,2,1,512,128]{4,3,2,1,0:T(8,128)(2,1)}, bf16[2,2,1,512,128]{4,3,2,1,0:T(8,128)(2,1)S(1)}, u32[]{:S(2)}, u32[]{:S(2)}) %collective-permute-start.7) | collective-permute-done | bytes 524320 | tf_op jit(solution)/shard_map/ppermute | solution.py:144
  101.0 0.2 collective-permute-done.8.refs_1_
  101.2 1.6 %place.5 = bf16[32,2,1,512,128]{4,3,2,1,0:T(8,128)(2,1)} custom-call(bf16[2,2,1,512,128]{4,3,2,1,0:T(8,128)(2,1)S(1)} %collective-permute-done.7.refs_0_, bf16[2,2,1,512,128]{4,3,2,1,0:T(8,128)(2,1)S(1)} %collective-permute-done.8.refs_1_, s32[16]{0:T(128)S(1)} %slice_bitcast_fusion.refs_7_.refs_3_.refs_2_, ...), custom_call_target="tpu_custom_call", output_to_operand_aliasing={{}: (3, {})} | custom-call | flops 1 | bytes 1 | tf_op jit(solution)/shard_map/place/pallas_call | solution.py:118
  (37 shorter events, 1.8 us)
Async XLA Ops:
  3.8 9.7 %copy-start.2 = (s32[32,2]{0,1:T(2,128)S(1)}, s32[32,2]{0,1:T(2,128)}, u32[]{:S(2)}) copy-start(s32[32,2]{0,1:T(2,128)} %param.8) | copy-start | bytes 772
  3.8 9.9 %copy-start = (bf16[4,16,128]{2,1,0:T(8,128)(2,1)S(1)}, bf16[4,16,128]{2,1,0:T(8,128)(2,1)}, u32[]{:S(2)}) copy-start(bf16[4,16,128]{2,1,0:T(8,128)(2,1)} %q_ref.1) | copy-start | bytes 49156
  3.9 9.9 %copy-start.1 = (s32[4]{0:T(128)S(1)}, s32[4]{0:T(128)}, u32[]{:S(2)}) copy-start(s32[4]{0:T(128)} %len_ref.3) | copy-start | bytes 52
  3.9 27.9 %collective-permute-start.2 = (bf16[8,2,1,512,128]{4,3,2,1,0:T(8,128)(2,1)}, bf16[8,2,1,512,128]{4,3,2,1,0:T(8,128)(2,1)}, u32[]{:S(2)}, u32[]{:S(2)}) collective-permute-start(bf16[8,2,1,512,128]{4,3,2,1,0:T(8,128)(2,1)} %gather.3), channel_id=1, source_target_pairs={{0,16},{1,65},{2,18},{3,67},{4,20},{5,69},{6,22},{7,71},{8,24},{9,... | collective-permute-start | bytes 6291464 | tf_op jit(solution)/shard_map/ppermute | solution.py:144
  12.0 43.7 %collective-permute-start.1 = (bf16[8,2,1,512,128]{4,3,2,1,0:T(8,128)(2,1)}, bf16[8,2,1,512,128]{4,3,2,1,0:T(8,128)(2,1)S(1)}, u32[]{:S(2)}, u32[]{:S(2)}) collective-permute-start(bf16[8,2,1,512,128]{4,3,2,1,0:T(8,128)(2,1)} %get-tuple-element.37), channel_id=1, source_target_pairs={{0,24},{1,97},{2,26},{3,99},{4,28},{5,101},{6,30},{7,103},{8,0},{9... | collective-permute-start | bytes 6291464 | tf_op jit(solution)/shard_map/ppermute | solution.py:144
  12.8 42.8 %collective-permute-start = (bf16[8,2,1,512,128]{4,3,2,1,0:T(8,128)(2,1)}, bf16[8,2,1,512,128]{4,3,2,1,0:T(8,128)(2,1)}, u32[]{:S(2)}, u32[]{:S(2)}) collective-permute-start(bf16[8,2,1,512,128]{4,3,2,1,0:T(8,128)(2,1)} %get-tuple-element.36), channel_id=1, source_target_pairs={{0,8},{1,33},{2,10},{3,35},{4,12},{5,37},{6,14},{7,39},{8,16},{9,4... | collective-permute-start | bytes 6291464 | tf_op jit(solution)/shard_map/ppermute | solution.py:144
  31.8 14.6 %copy-start.3 = (s32[4]{0:T(128)S(1)}, s32[4]{0:T(128)}, u32[]{:S(2)}) copy-start(s32[4]{0:T(128)} %param.11) | copy-start | bytes 52
  39.6 21.0 %all-to-all-start = ((f32[16,1,640]{2,1,0:T(1,128)}), f32[16,1,640]{2,1,0:T(1,128)S(1)}, u32[]{:S(2)}, u32[]{:S(2)}) async-start(f32[16,1,640]{2,1,0:T(1,128)} %attend_late.1), calls=%async_computation | async-start | bytes 81920 | tf_op jit(solution)/shard_map/all_to_all | solution.py:294
  50.0 17.1 %collective-permute-start.3 = (bf16[4,2,1,512,128]{4,3,2,1,0:T(8,128)(2,1)}, bf16[4,2,1,512,128]{4,3,2,1,0:T(8,128)(2,1)S(1)}, u32[]{:S(2)}, u32[]{:S(2)}) collective-permute-start(bf16[4,2,1,512,128]{4,3,2,1,0:T(8,128)(2,1)} %get-tuple-element.47), channel_id=1, source_target_pairs={{0,64},{1,17},{2,66},{3,19},{4,68},{5,21},{6,70},{7,23},{8,72},{9,... | collective-permute-start | bytes 3145736 | tf_op jit(solution)/shard_map/ppermute | solution.py:144
  53.0 25.3 %collective-permute-start.4 = (bf16[4,2,1,512,128]{4,3,2,1,0:T(8,128)(2,1)}, bf16[4,2,1,512,128]{4,3,2,1,0:T(8,128)(2,1)}, u32[]{:S(2)}, u32[]{:S(2)}) collective-permute-start(bf16[4,2,1,512,128]{4,3,2,1,0:T(8,128)(2,1)} %get-tuple-element.48), channel_id=1, source_target_pairs={{0,32},{1,9},{2,34},{3,11},{4,36},{5,13},{6,38},{7,15},{8,40},{9,1... | collective-permute-start | bytes 3145736 | tf_op jit(solution)/shard_map/ppermute | solution.py:144
  53.3 25.2 %collective-permute-start.5 = (bf16[4,2,1,512,128]{4,3,2,1,0:T(8,128)(2,1)}, bf16[4,2,1,512,128]{4,3,2,1,0:T(8,128)(2,1)}, u32[]{:S(2)}, u32[]{:S(2)}) collective-permute-start(bf16[4,2,1,512,128]{4,3,2,1,0:T(8,128)(2,1)} %get-tuple-element.49), channel_id=1, source_target_pairs={{0,96},{1,25},{2,98},{3,27},{4,100},{5,29},{6,102},{7,31},{8,104},... | collective-permute-start | bytes 3145736 | tf_op jit(solution)/shard_map/ppermute | solution.py:144
  58.5 31.2 %collective-permute-start.6 = (bf16[4,2,1,512,128]{4,3,2,1,0:T(8,128)(2,1)}, bf16[4,2,1,512,128]{4,3,2,1,0:T(8,128)(2,1)}, u32[]{:S(2)}, u32[]{:S(2)}) collective-permute-start(bf16[4,2,1,512,128]{4,3,2,1,0:T(8,128)(2,1)} %get-tuple-element.52), channel_id=1, source_target_pairs={{0,64},{1,17},{2,66},{3,19},{4,68},{5,21},{6,70},{7,23},{8,72},{9,... | collective-permute-start | bytes 3145736 | tf_op jit(solution)/shard_map/ppermute | solution.py:144
  62.3 31.1 %all-to-all-start.1 = ((f32[16,4,128]{2,1,0:T(4,128)}), f32[16,4,128]{2,1,0:T(4,128)S(1)}, u32[]{:S(2)}, u32[]{:S(2)}) async-start(f32[16,4,128]{2,1,0:T(4,128)} %broadcast_in_dim.47), calls=%async_computation.1 | async-start | bytes 65536 | tf_op jit(solution)/shard_map/all_to_all | solution.py:320
  78.4 17.0 %collective-permute-start.9 = (bf16[2,2,1,512,128]{4,3,2,1,0:T(8,128)(2,1)}, bf16[2,2,1,512,128]{4,3,2,1,0:T(8,128)(2,1)}, u32[]{:S(2)}, u32[]{:S(2)}) collective-permute-start(bf16[2,2,1,512,128]{4,3,2,1,0:T(8,128)(2,1)} %get-tuple-element.66), channel_id=1, source_target_pairs={{0,32},{1,9},{2,34},{3,11},{4,36},{5,13},{6,38},{7,15},{8,40},{9,1... | collective-permute-start | bytes 1572872 | tf_op jit(solution)/shard_map/ppermute | solution.py:144
  79.6 16.1 %collective-permute-start.10 = (bf16[2,2,1,512,128]{4,3,2,1,0:T(8,128)(2,1)}, bf16[2,2,1,512,128]{4,3,2,1,0:T(8,128)(2,1)}, u32[]{:S(2)}, u32[]{:S(2)}) collective-permute-start(bf16[2,2,1,512,128]{4,3,2,1,0:T(8,128)(2,1)} %get-tuple-element.67), channel_id=1, source_target_pairs={{0,96},{1,25},{2,98},{3,27},{4,100},{5,29},{6,102},{7,31},{8,104},... | collective-permute-start | bytes 1572872 | tf_op jit(solution)/shard_map/ppermute | solution.py:144
  89.7 11.3 %collective-permute-start.7 = (bf16[2,2,1,512,128]{4,3,2,1,0:T(8,128)(2,1)}, bf16[2,2,1,512,128]{4,3,2,1,0:T(8,128)(2,1)S(1)}, u32[]{:S(2)}, u32[]{:S(2)}) collective-permute-start(bf16[2,2,1,512,128]{4,3,2,1,0:T(8,128)(2,1)} %get-tuple-element.63), channel_id=1, source_target_pairs={{0,32},{1,9},{2,34},{3,11},{4,36},{5,13},{6,38},{7,15},{8,40},{9,1... | collective-permute-start | bytes 1572872 | tf_op jit(solution)/shard_map/ppermute | solution.py:144
  91.0 10.2 %collective-permute-start.8 = (bf16[2,2,1,512,128]{4,3,2,1,0:T(8,128)(2,1)}, bf16[2,2,1,512,128]{4,3,2,1,0:T(8,128)(2,1)S(1)}, u32[]{:S(2)}, u32[]{:S(2)}) collective-permute-start(bf16[2,2,1,512,128]{4,3,2,1,0:T(8,128)(2,1)} %get-tuple-element.64), channel_id=1, source_target_pairs={{0,96},{1,25},{2,98},{3,27},{4,100},{5,29},{6,102},{7,31},{8,104},... | collective-permute-start | bytes 1572872 | tf_op jit(solution)/shard_map/ppermute | solution.py:144
